TPU v7x, 128 devices: a whole 4x4x4 slice. The times are simulated.
128 devices in a mesh: seq: 2 (over y_hi), fsdp: 64 (over y_lo, x, z, core).
Axes of the slice: x: 4, y: 4 (y_hi: 2, y_lo: 2; y = y_hi * 2 + y_lo), z: 4, core: 2. Of those that a mesh axis runs over, the one named last changes fastest.
Arguments:
- tokens: bfloat16 [64, 256, 1024], P('fsdp', 'seq'), may hold values from -6 to 6
- positions: int32 [64, 256], P('fsdp', 'seq'), may hold values from 0 to 765, as said below
- routes: int32 [64, 256, 8], P('fsdp', 'seq'), may hold values from 0 to 31, all different within a row; in each aligned block of 128 rows (0 to 127, 128 to 255, ..., all dimensions but the last counted through in order) at most 44 rows name the same one
- cotangent: bfloat16 [64, 256, 1024], P('fsdp', 'seq'), may hold values from -6 to 6
- first_gain: bfloat16 [1024], P('fsdp'), may hold values from 0.099609375 to 1.8984375
- w_query: bfloat16 [1024, 1024], P('fsdp'), may hold values from -0.1875 to 0.1875
- w_key: bfloat16 [1024, 512], P('fsdp'), may hold values from -0.1875 to 0.1875
- w_value: bfloat16 [1024, 512], P('fsdp'), may hold values from -0.1875 to 0.1875
- w_out: bfloat16 [1024, 1024], P('fsdp'), may hold values from -0.75 to 0.75
- second_gain: bfloat16 [1024], P('fsdp'), may hold values from 0.099609375 to 1.8984375
- w_router: bfloat16 [1024, 32], P('fsdp'), may hold values from -0.09375 to 0.09375
- w_gate: bfloat16 [64, 512, 512], P('fsdp'), may hold values from -0.1875 to 0.1875
- w_up: bfloat16 [64, 512, 512], P('fsdp'), may hold values from -0.1875 to 0.1875
- w_down: bfloat16 [64, 256, 1024], P('fsdp'), may hold values from -0.75 to 0.75
Outputs:
- layer_out: bfloat16 [64, 256, 1024], P('fsdp', 'seq')
- grad_tokens: float32 [64, 256, 1024], P('fsdp', 'seq')
- grad_first_gain: float32 [1024], P('fsdp')
- grad_query: float32 [1024, 1024], P('fsdp')
- grad_key: float32 [1024, 512], P('fsdp')
- grad_value: float32 [1024, 512], P('fsdp')
- grad_out: float32 [1024, 1024], P('fsdp')
- grad_second_gain: float32 [1024], P('fsdp')
- grad_router: float32 [1024, 32], P('fsdp')
- grad_gate: float32 [64, 512, 512], P('fsdp')
- grad_up: float32 [64, 512, 512], P('fsdp')
- grad_down: float32 [64, 256, 1024], P('fsdp')
Inputs may be any that keep to these rules, and one draw needn't show every extreme that they name: `positions`: each sequence starts at position 0; each next token's position is 1 to 3 larger, except that the last token of every sequence stands at position 765. `routes`: A row names 8 different experts. Among the 128 rows of one device (aligned blocks of a sequence), no expert is named by more than 44 rows, a bound that some block reaches.
All inputs are finite; a program needn't handle non-finite values.
Results may differ from a plain program's by a relative error of at most 0.017.
Values may be sent and summed in bfloat16 or wider, within the bound.
A program may use at most 128 MiB of HBM per device.

v0:
```python
import functools

import jax
import jax.numpy as jnp
from jax import lax
from jax.experimental import pallas as pl
from jax.experimental.pallas import tpu as pltpu
from jax.sharding import PartitionSpec as P

HD = 64
CORES = 2
SMALL = 128

epsilon = 1e-06
rope_base = 10000.0
masked_score = -1e30
MESH = pl.DeviceIdType.MESH
ANY = pl.BlockSpec(memory_space=pl.ANY)
VMEM = pl.BlockSpec(memory_space=pltpu.VMEM)


def dot_plain(left, right):
    return jnp.dot(left, right, preferred_element_type=jnp.float32)


def dot_left(left, right):
    return lax.dot_general(
        left, right, (((0,), (0,)), ((), ())), preferred_element_type=jnp.float32
    )


def dot_right(left, right):
    return lax.dot_general(
        left, right, (((1,), (1,)), ((), ())), preferred_element_type=jnp.float32
    )


def rms_scale(values, gain):
    return values * lax.rsqrt(jnp.mean(values * values, axis=-1, keepdims=True) + epsilon) * gain


def in_two(values):
    high = lax.reduce_precision(values, 8, 7)
    return high.astype(jnp.bfloat16), (values - high).astype(jnp.bfloat16)


def rotate(values, cosine, sine_table):
    middle = values.shape[-1] // 2
    first_half = values[..., :middle]
    second_half = values[..., middle:]
    return jnp.concatenate(
        [
            first_half * cosine - second_half * sine_table,
            second_half * cosine + first_half * sine_table,
        ],
        axis=-1,
    )


LONG = 4


def coordinates():
    seq, me = lax.axis_index("seq"), lax.axis_index("fsdp")
    return seq, me // 32, (me // 8) % LONG, (me // 2) % LONG, me % CORES


def device(seq, y, x, z, core):
    return (seq, ((y * LONG + x) * LONG + z) * CORES + core)


def enter(targets):
    barrier = pltpu.get_barrier_semaphore()
    for target in targets:
        pl.semaphore_signal(barrier, inc=1, device_id=target, device_id_type=MESH)
    pl.semaphore_wait(barrier, len(targets))


def neighbours():
    seq, y, x, z, core = coordinates()
    return [
        device(seq, y, x, z, 1 - core),
        device(seq, 1 - y, x, z, core),
        device(seq, y, lax.rem(x + 1, LONG), z, core),
        device(seq, y, lax.rem(x + 3, LONG), z, core),
        device(seq, y, x, lax.rem(z + 1, LONG), core),
        device(seq, y, x, lax.rem(z + 3, LONG), core),
        device(1 - seq, y, x, z, core),
    ]


def gather_kernel(shard_a, shard_b, x_own, pos_own, full_a, full_b, x_other, pos_other, *sems):
    send, recv, core_send, core_recv, seq_send, seq_recv, local = sems
    seq, y, x, z, core = coordinates()
    enter(neighbours())
    other_seq = device(1 - seq, y, x, z, core)
    swaps = [
        pltpu.make_async_remote_copy(
            src_ref=source,
            dst_ref=target,
            send_sem=seq_send.at[i],
            recv_sem=seq_recv.at[i],
            device_id=other_seq,
            device_id_type=MESH,
        )
        for i, (source, target) in enumerate(((x_own, x_other), (pos_own, pos_other)))
    ]
    fulls = (full_a, full_b)
    first_at, second_at = (x, z), (z, x)

    def along(i, stage, shift):
        if (i == 0) == (stage == 0):
            return device(seq, y, lax.rem(x + shift, LONG), z, core)
        return device(seq, y, x, lax.rem(z + shift, LONG), core)

    def block(i, stage, shift, ys):
        at = lax.rem((first_at if stage == 0 else second_at)[i] + shift, LONG)
        if stage == 0:
            xs, zs = (at, z) if i == 0 else (x, at)
        else:
            xs, zs = (slice(None), at) if i == 0 else (at, slice(None))
        return fulls[i].at[ys, xs, zs, core]

    def copy(i, k, part, target):
        return pltpu.make_async_remote_copy(
            src_ref=part,
            dst_ref=part,
            send_sem=send.at[i, k],
            recv_sem=recv.at[i, k],
            device_id=target,
            device_id_type=MESH,
        )

    both = slice(None)
    own = []
    started = []

    def start(i, k, part, target):
        moved = copy(i, k, part, target)
        moved.start()
        started.append(moved)

    crossing = []

    def cross(i, k, index):
        for side, wait in ((core, False), (1 - core, True)):
            part = fulls[i].at[(*index, side)]
            moved = pltpu.make_async_remote_copy(
                src_ref=part,
                dst_ref=part,
                send_sem=core_send.at[i, k],
                recv_sem=core_recv.at[i, k],
                device_id=device(seq, y, x, z, 1 - core),
                device_id_type=MESH,
            )
            if wait:
                crossing.append((moved, last))
            else:
                moved.start()
                last = moved

    for i, shard in enumerate((shard_a, shard_b)):
        kept = pltpu.make_async_copy(shard, fulls[i].at[y, x, z, core], local.at[i])
        kept.start()
        own.append(kept)
        outgoing = pltpu.make_async_remote_copy(
            src_ref=shard,
            dst_ref=fulls[i].at[y, x, z, core],
            send_sem=send.at[i, 0],
            recv_sem=recv.at[i, 0],
            device_id=device(seq, 1 - y, x, z, core),
            device_id_type=MESH,
        )
        outgoing.start()
        started.append(outgoing)
    for moved in swaps:
        moved.start()
    for i in range(2):
        own[i].wait()
        copy(i, 0, fulls[i].at[1 - y, x, z, core], other_seq).wait_recv()

    for stage in range(2):
        base = 1 + 4 * stage
        for i in range(2):
            start(i, base, block(i, stage, 0, both), along(i, stage, 1))
            start(i, base + 1, block(i, stage, 0, both), along(i, stage, 3))
            if stage == 1:
                at = second_at[i]
                cross(i, 0, (both, both, at) if i == 0 else (both, at, both))
        for i in range(2):
            copy(i, base, block(i, stage, 3, both), other_seq).wait_recv()
            start(i, base + 2, block(i, stage, 3, 0), along(i, stage, 1))
            copy(i, base + 1, block(i, stage, 1, both), other_seq).wait_recv()
            start(i, base + 3, block(i, stage, 1, 1), along(i, stage, 3))
            if stage == 1:
                for k, shift in ((1, 3), (2, 1)):
                    at = lax.rem(second_at[i] + shift, LONG)
                    cross(i, k, (both, both, at) if i == 0 else (both, at, both))
        for i in range(2):
            copy(i, base + 2, block(i, stage, 2, 0), other_seq).wait_recv()
            copy(i, base + 3, block(i, stage, 2, 1), other_seq).wait_recv()
            if stage == 1:
                at = lax.rem(second_at[i] + 2, LONG)
                cross(i, 3, (both, both, at) if i == 0 else (both, at, both))

    for arriving, leaving in crossing:
        arriving.wait_recv()
        leaving.wait_send()
    for moved in started:
        moved.wait_send()
    for moved in swaps:
        moved.wait()


def gather_shards(shard_a, shard_b, x_own, pos_own):
    count = lax.axis_size("fsdp")
    chips = (count // (LONG * LONG * CORES), LONG, LONG, CORES)
    shards = (shard_a, shard_b)
    outs = [jax.ShapeDtypeStruct((*chips, *shard.shape), shard.dtype) for shard in shards]
    outs += [jax.ShapeDtypeStruct(array.shape, array.dtype) for array in (x_own, pos_own)]
    full_a, full_b, x_other, pos_other = pl.pallas_call(
        gather_kernel,
        out_shape=outs,
        in_specs=[ANY] * 4,
        out_specs=[ANY] * 4,
        scratch_shapes=[
            pltpu.SemaphoreType.DMA((2, 9)),
            pltpu.SemaphoreType.DMA((2, 9)),
            pltpu.SemaphoreType.DMA((2, 4)),
            pltpu.SemaphoreType.DMA((2, 4)),
            pltpu.SemaphoreType.DMA((2,)),
            pltpu.SemaphoreType.DMA((2,)),
            pltpu.SemaphoreType.DMA((2,)),
        ],
        compiler_params=pltpu.CompilerParams(collective_id=0, has_side_effects=True),
        name="gather_weights",
    )(shard_a, shard_b, x_own, pos_own)
    height = count * shard_a.shape[0]
    return (
        full_a.reshape(height, shard_a.shape[1]),
        full_b.reshape(height, shard_b.shape[1]),
        x_other,
        pos_other,
    )


def widen(values):
    return values.astype(jnp.float32)


def scatter_kernel(groups, *refs):
    number = len(groups)
    parts, totals = refs[:number], refs[number : 2 * number]
    halves, landed, second, landed_two, third, landed_three = (
        refs[k * number : (k + 1) * number] for k in range(2, 8)
    )
    core_send, core_recv, send, recv = refs[8 * number :]
    seq, y, x, z, core = coordinates()
    far_y = [
        device(seq, 1 - y, x, z, core),
        device(1 - seq, y, x, z, core),
        device(1 - seq, 1 - y, x, z, core),
    ]
    lines = [
        [device(seq, y, lax.rem(x + j, LONG), z, core) for j in (1, 2, 3)],
        [device(seq, y, x, lax.rem(z + j, LONG), core) for j in (1, 2, 3)],
    ]
    enter([device(seq, y, x, z, 1 - core)] + far_y + lines[0] + lines[1])

    def index(i, at):
        return (slice(None), slice(None), at) if groups[i] == 0 else (slice(None), at)

    first_at = [z if group == 0 else x for group in groups]
    second_at = [x if group == 0 else z for group in groups]
    first_line = [lines[1] if group == 0 else lines[0] for group in groups]
    second_line = [lines[0] if group == 0 else lines[1] for group in groups]

    def remote(source, target, to, sems, i, k):
        return pltpu.make_async_remote_copy(
            src_ref=source,
            dst_ref=target,
            send_sem=sems[0].at[i, k],
            recv_sem=sems[1].at[i, k],
            device_id=to,
            device_id_type=MESH,
        )

    def part_of(i, at, side):
        if groups[i] == 0:
            return parts[i].at[:, :, at, side]
        return parts[i].at[:, at, :, side]

    order = (2, 1, 3, 0)
    waiting = []
    across = {}
    for j in order:
        for i in range(number):
            at = lax.rem(first_at[i] + j, LONG)
            moved = remote(
                part_of(i, at, 1 - core),
                halves[i].at[j],
                device(seq, y, x, z, 1 - core),
                (core_send, core_recv),
                i,
                j,
            )
            moved.start()
            across[i, j] = moved
    for j in order:
        for i in range(number):
            across[i, j].wait_recv()
            at = lax.rem(first_at[i] + j, LONG)
            both = widen(halves[i][j]) + widen(part_of(i, at, core)[...])
            halves[i][j] = both.astype(jnp.bfloat16)
            if j:
                moved = remote(
                    halves[i].at[j],
                    landed[i].at[j - 1],
                    first_line[i][j - 1],
                    (send, recv),
                    i,
                    j - 1,
                )
                moved.start()
                waiting.append(moved)
    hops = {}
    for i in range(number):
        for j in (1, 2, 3):
            remote(halves[i].at[j], landed[i].at[j - 1], far_y[0], (send, recv), i, j - 1).wait_recv()
        total = widen(halves[i][0])
        for j in range(3):
            total = total + widen(landed[i][j])
        second[i][...] = total.astype(jnp.bfloat16)
        for j in (2, 1, 3):
            at = lax.rem(second_at[i] + j, LONG)
            moved = remote(
                second[i].at[:, at],
                landed_two[i].at[j - 1],
                second_line[i][j - 1],
                (send, recv),
                i,
                2 + j,
            )
            moved.start()
            waiting.append(moved)
            hops[i, j] = moved
    for i in range(number):
        for j in (1, 2, 3):
            hops[i, j].wait_recv()
        total = widen(second[i][:, second_at[i]])
        for j in range(3):
            total = total + widen(landed_two[i][j])
        third[i][...] = total.astype(jnp.bfloat16)
        landed_three[i][seq * 2 + y] = third[i][y]
        for k, wanted in enumerate((1 - y, y, 1 - y)):
            moved = remote(
                third[i].at[wanted],
                landed_three[i].at[seq * 2 + y],
                far_y[k],
                (send, recv),
                i,
                6 + k,
            )
            moved.start()
            waiting.append(moved)
            hops[i, 3 + k] = moved
    for i in range(number):
        for k in range(3):
            hops[i, 3 + k].wait_recv()
        total = widen(landed_three[i][0])
        for k in range(1, 4):
            total = total + widen(landed_three[i][k])
        totals[i][...] = total
    for moved in waiting:
        moved.wait_send()
    for i in range(number):
        for j in order:
            across[i, j].wait_send()


def scatter_sums(fulls, groups, identity):
    count = lax.axis_size("fsdp")
    number = len(fulls)
    rows = fulls[0].shape[0] // count
    widths = [full.shape[1] for full in fulls]
    ys = count // (LONG * LONG * CORES)
    parts = [full.reshape(ys, LONG, LONG, CORES, rows, full.shape[1]) for full in fulls]

    def room(*lead):
        return [pltpu.VMEM((*lead, rows, width), jnp.bfloat16) for width in widths]

    return pl.pallas_call(
        functools.partial(scatter_kernel, groups),
        out_shape=[jax.ShapeDtypeStruct((rows, width), jnp.float32) for width in widths],
        in_specs=[VMEM] * number,
        out_specs=[VMEM] * number,
        scratch_shapes=room(LONG, ys, LONG)
        + room(LONG - 1, ys, LONG)
        + room(ys, LONG)
        + room(LONG - 1, ys)
        + room(ys)
        + room(2 * ys)
        + [
            pltpu.SemaphoreType.DMA((number, LONG)),
            pltpu.SemaphoreType.DMA((number, LONG)),
            pltpu.SemaphoreType.DMA((number, 9)),
            pltpu.SemaphoreType.DMA((number, 9)),
        ],
        compiler_params=pltpu.CompilerParams(
            collective_id=identity, has_side_effects=True, vmem_limit_bytes=48 * 2**20
        ),
        name="scatter_gradients",
    )(*parts)


CHUNKS = 4
SAME, CROSS = 32, 16
BLOCK = SAME + CROSS


def chip_at(sign, step):
    seq, y, x, z, core = coordinates()
    chunk, inner = step // 8, step % 8
    dy, dx = inner // LONG, inner % LONG
    dz = (dx + chunk) % LONG
    return ((y + dy) % 2 * LONG + (x + sign * dx + LONG) % LONG) * LONG + (
        z + sign * dz + LONG
    ) % LONG


def expert_kernel(
    onehot,
    gates,
    normed,
    grad_low,
    own_gate,
    own_up,
    own_down,
    out_ref,
    back_ref,
    dots_ref,
    d_gate,
    d_up,
    d_down,
    picks,
    x_send,
    g_send,
    x_land,
    g_land,
    out_rows,
    back_land,
    gate_pre,
    up_pre,
    hidden,
    d_gate_pre,
    d_up_pre,
    w_gate,
    w_up,
    w_down,
    pair_send,
    pair_land,
    pair_send_down,
    pair_land_down,
    seq_send,
    seq_land,
    seq_send_down,
    seq_land_down,
    x_sems,
    g_sems,
    back_sems,
    self_sems,
    out_sems,
    weight_sems,
    sum_sems,
):
    seq, y, x, z, core = coordinates()
    me = lax.axis_index("fsdp")
    width = normed.shape[1]
    chips = onehot.shape[0]
    steps = chips // CHUNKS
    depth = steps * BLOCK
    partner = (seq, me + 1 - 2 * core)
    other_seq = (1 - seq, me)

    barrier = pltpu.get_barrier_semaphore()
    for target in (partner, other_seq):
        pl.semaphore_signal(barrier, inc=1, device_id=target, device_id_type=MESH)

    @pl.loop(1, chips)
    def _(step):
        for side in range(CORES):
            pl.semaphore_signal(
                barrier,
                inc=1,
                device_id=(seq, chip_at(-1, step) * CORES + side),
                device_id_type=MESH,
            )

    pl.semaphore_wait(barrier, CORES * chips)

    def remote(source, target, sends, recvs, to):
        return pltpu.make_async_remote_copy(
            src_ref=source,
            dst_ref=target,
            send_sem=sends,
            recv_sem=recvs,
            device_id=to,
            device_id_type=MESH,
        )

    weights = []
    for i, (own, full) in enumerate(((own_gate, w_gate), (own_up, w_up), (own_down, w_down))):
        height = own.shape[0]
        place = full.at[pl.ds(pl.multiple_of(core * height, height), height)]
        kept = pltpu.make_async_copy(own, place, weight_sems.at[2, i])
        sent = remote(own, place, weight_sems.at[0, i], weight_sems.at[1, i], partner)
        kept.start()
        sent.start()
        weights.append((kept, sent))

    def send_block(source, target, sems, kind, sign, step):
        chip = chip_at(sign, step)
        chunk = step // steps
        row = pl.multiple_of(step * BLOCK, 16)
        same, cross = pl.ds(row, SAME), pl.ds(pl.multiple_of(row + SAME, 16), CROSS)

        @pl.when(step == 0)
        def _():
            pltpu.make_async_copy(source.at[same], target.at[same], self_sems.at[kind]).start()

        @pl.when(step > 0)
        def _():
            remote(
                source.at[same],
                target.at[same],
                sems.at[0, chunk],
                sems.at[1, chunk],
                (seq, chip * CORES + core),
            ).start()

        remote(
            source.at[cross],
            target.at[cross],
            sems.at[0, chunk],
            sems.at[1, chunk],
            (seq, chip * CORES + 1 - core),
        ).start()

    def whole(buffer, sems, chunk, first):
        rows = pl.ds(SAME, depth - SAME) if first else pl.ds(pl.multiple_of(chunk * depth, 16), depth)
        part = buffer.at[rows]
        return remote(part, part, sems.at[0, chunk], sems.at[1, chunk], partner)

    def wait_chunk(source, target, sems, kind, chunk):
        @pl.when(chunk == 0)
        def _():
            pltpu.make_async_copy(
                source.at[pl.ds(0, SAME)], target.at[pl.ds(0, SAME)], self_sems.at[kind]
            ).wait()
            whole(target, sems, 0, True).wait_recv()

        @pl.when(chunk > 0)
        def _():
            whole(target, sems, chunk, False).wait_recv()

    def wait_sends(source, sems):
        for chunk in range(CHUNKS):
            whole(source, sems, chunk, chunk == 0).wait_send()

    @pl.loop(0, chips)
    def _(step):
        chip = chip_at(1, step)
        rows = pl.ds(pl.multiple_of(step * BLOCK, 16), BLOCK)
        picks[rows, :] = onehot[chip]
        x_send[rows, width:] = gates[chip]

    for values, buffer, target, sems, kind in (
        (normed, x_send, x_land, x_sems, 0),
        (grad_low, g_send, g_land, g_sems, 1),
    ):

        @pl.loop(0, CHUNKS)
        def _(chunk):
            rows = pl.ds(pl.multiple_of(chunk * depth, 16), depth)
            buffer[rows, :width] = dot_plain(picks[rows, :], values[...]).astype(jnp.bfloat16)

            @pl.loop(0, steps)
            def _(inner):
                send_block(buffer, target, sems, kind, 1, chunk * steps + inner)

    for kept, sent in weights:
        kept.wait()
        sent.wait()

    @pl.loop(0, CHUNKS)
    def _(chunk):
        rows = pl.ds(pl.multiple_of(chunk * depth, 16), depth)
        wait_chunk(x_send, x_land, x_sems, 0, chunk)
        served = x_land[rows, :width]
        gate = dot_plain(served, w_gate[...])
        up = dot_plain(served, w_up[...])
        gate_pre[rows, :] = gate
        up_pre[rows, :] = up
        low = (gate * jax.nn.sigmoid(gate) * up).astype(jnp.bfloat16)
        hidden[rows, :] = low
        out_rows[rows, :] = dot_plain(low, w_down[...]).astype(jnp.bfloat16)

        @pl.loop(0, steps)
        def _(inner):
            step = chunk * steps + inner
            row = pl.multiple_of(step * BLOCK, 16)
            chip = chip_at(-1, step)
            out_ref[chip, :SAME, :] = out_rows[pl.ds(row, SAME), :]
            remote(
                out_rows.at[pl.ds(pl.multiple_of(row + SAME, 16), CROSS)],
                out_ref.at[chip, pl.ds(SAME, CROSS)],
                out_sems.at[0],
                out_sems.at[1],
                partner,
            ).start()

    wait_sends(x_send, x_sems)

    @pl.loop(0, CHUNKS)
    def _(chunk):
        rows = pl.ds(pl.multiple_of(chunk * depth, 16), depth)
        wait_chunk(g_send, g_land, g_sems, 1, chunk)
        grads = g_land[rows, :].astype(jnp.float32)
        dots = jnp.sum(grads * out_rows[rows, :].astype(jnp.float32), axis=1, keepdims=True)
        high = dots.astype(jnp.bfloat16).astype(jnp.float32)
        lane = lax.broadcasted_iota(jnp.int32, (depth, SMALL), 1)
        x_send[rows, width:] = jnp.where(
            lane == 0, high, jnp.where(lane == 1, dots - high, 0.0)
        ).astype(jnp.bfloat16)
        weight = jnp.sum(x_land[rows, width:].astype(jnp.float32), axis=1, keepdims=True)
        low = (weight * grads).astype(jnp.bfloat16)
        g_land[rows, :] = low
        d_hidden = dot_right(low, w_down[...])
        gate, up = gate_pre[rows, :], up_pre[rows, :]
        sigmoid = jax.nn.sigmoid(gate)
        one = (d_hidden * up * sigmoid * (1.0 + gate * (1.0 - sigmoid))).astype(jnp.bfloat16)
        two = (d_hidden * (gate * sigmoid)).astype(jnp.bfloat16)
        d_gate_pre[rows, :] = one
        d_up_pre[rows, :] = two
        x_send[rows, :width] = (dot_right(one, w_gate[...]) + dot_right(two, w_up[...])).astype(
            jnp.bfloat16
        )

        @pl.loop(0, steps)
        def _(inner):
            send_block(x_send, back_land, back_sems, 2, -1, chunk * steps + inner)

    tile = 256
    half = own_gate.shape[0]
    half_down = own_down.shape[0]

    def product(side, which, at):
        start = pl.multiple_of(side * half + at * tile, tile)
        return dot_left(x_land[:, pl.ds(start, tile)], (d_gate_pre, d_up_pre)[which][...])

    def product_down(side, at):
        start = pl.multiple_of(side * half_down, half_down)
        columns = pl.ds(pl.multiple_of(at * half, half), half)
        return dot_left(hidden[:, pl.ds(start, half_down)], g_land[:, columns]), columns

    def both_tiles(side, keep):
        @pl.loop(0, half // tile)
        def _(at):
            for which in range(2):
                keep(which, pl.ds(pl.multiple_of(at * tile, tile), tile), product(side, which, at))

    def keep_other(which, rows, values):
        pair_send[which, rows, :] = values.astype(jnp.bfloat16)

    def keep_own(which, rows, values):
        (d_gate, d_up)[which][rows, :] = values

    both_tiles(1 - core, keep_other)

    @pl.loop(0, width // half)
    def _(at):
        values, columns = product_down(1 - core, at)
        pair_send_down[:, columns] = values.astype(jnp.bfloat16)

    pairs = [
        remote(pair_send, pair_land, sum_sems.at[0, 0], sum_sems.at[1, 0], partner),
        remote(pair_send_down, pair_land_down, sum_sems.at[0, 1], sum_sems.at[1, 1], partner),
    ]
    for moved in pairs:
        moved.start()
    both_tiles(core, keep_own)

    @pl.loop(0, width // half)
    def _(at):
        values, columns = product_down(core, at)
        d_down[:, columns] = values

    pairs[0].wait_recv()
    for which, mine in enumerate((d_gate, d_up)):
        seq_send[which] = (mine[...] + pair_land[which].astype(jnp.float32)).astype(jnp.bfloat16)
    pairs[1].wait_recv()
    seq_send_down[...] = (d_down[...] + pair_land_down[...].astype(jnp.float32)).astype(
        jnp.bfloat16
    )
    sums = [
        remote(seq_send, seq_land, sum_sems.at[0, 2], sum_sems.at[1, 2], other_seq),
        remote(seq_send_down, seq_land_down, sum_sems.at[0, 3], sum_sems.at[1, 3], other_seq),
    ]
    for moved in sums:
        moved.start()

    back_ref[...] = jnp.zeros_like(back_ref)

    @pl.loop(0, CHUNKS)
    def _(chunk):
        rows = pl.ds(pl.multiple_of(chunk * depth, 16), depth)
        wait_chunk(x_send, back_land, back_sems, 2, chunk)
        back_ref[...] += dot_left(picks[rows, :], back_land[rows, :width])

    @pl.loop(0, chips)
    def _(step):
        rows = pl.ds(pl.multiple_of(step * BLOCK, 16), BLOCK)
        dots_ref[chip_at(1, step)] = back_land[rows, width:]

    sums[0].wait_recv()
    for which, mine in enumerate((d_gate, d_up)):
        mine[...] = seq_send[which].astype(jnp.float32) + seq_land[which].astype(jnp.float32)
    sums[1].wait_recv()
    d_down[...] = seq_send_down[...].astype(jnp.float32) + seq_land_down[...].astype(jnp.float32)
    outs = out_rows.at[pl.ds(0, chips * CROSS)]
    remote(outs, outs, out_sems.at[0], out_sems.at[1], partner).wait()
    wait_sends(g_send, g_sems)
    wait_sends(x_send, back_sems)
    for moved in pairs + sums:
        moved.wait_send()


def run_experts(onehot, gates, normed, grad_low, own_gate, own_up, own_down):
    chips, _, rows = onehot.shape
    width, hidden = normed.shape[1], own_gate.shape[1]
    slots = chips * BLOCK
    low, high = jnp.bfloat16, jnp.float32
    dma = pltpu.SemaphoreType.DMA
    half, half_down = own_gate.shape[0], own_down.shape[0]
    return pl.pallas_call(
        expert_kernel,
        out_shape=[
            jax.ShapeDtypeStruct((chips, BLOCK, width), low),
            jax.ShapeDtypeStruct((rows, width), high),
            jax.ShapeDtypeStruct((chips, BLOCK, SMALL), low),
            jax.ShapeDtypeStruct(own_gate.shape, high),
            jax.ShapeDtypeStruct(own_up.shape, high),
            jax.ShapeDtypeStruct(own_down.shape, high),
        ],
        in_specs=[VMEM] * 7,
        out_specs=[VMEM] * 6,
        scratch_shapes=[
            pltpu.VMEM((slots, rows), low),
            pltpu.VMEM((slots, width + SMALL), low),
            pltpu.VMEM((slots, width), low),
            pltpu.VMEM((slots, width + SMALL), low),
            pltpu.VMEM((slots, width), low),
            pltpu.VMEM((slots, width), low),
            pltpu.VMEM((slots, width + SMALL), low),
            pltpu.VMEM((slots, hidden), high),
            pltpu.VMEM((slots, hidden), high),
            pltpu.VMEM((slots, hidden), low),
            pltpu.VMEM((slots, hidden), low),
            pltpu.VMEM((slots, hidden), low),
            pltpu.VMEM((CORES * half, hidden), low),
            pltpu.VMEM((CORES * half, hidden), low),
            pltpu.VMEM((CORES * half_down, width), low),
            pltpu.VMEM((2, half, hidden), low),
            pltpu.VMEM((2, half, hidden), low),
            pltpu.VMEM((half_down, width), low),
            pltpu.VMEM((half_down, width), low),
            pltpu.VMEM((2, half, hidden), low),
            pltpu.VMEM((2, half, hidden), low),
            pltpu.VMEM((half_down, width), low),
            pltpu.VMEM((half_down, width), low),
            dma((2, CHUNKS)),
            dma((2, CHUNKS)),
            dma((2, CHUNKS)),
            dma((3,)),
            dma((2,)),
            dma((3, 3)),
            dma((2, 4)),
        ],
        compiler_params=pltpu.CompilerParams(
            collective_id=2, has_side_effects=True, vmem_limit_bytes=60 * 2**20
        ),
        name="experts",
    )(onehot, gates, normed, grad_low, own_gate, own_up, own_down)


def from_experts(blocks):
    groups = [
        [chip * CORES + core for chip in range(blocks.shape[0])] for core in range(CORES)
    ]
    return lax.all_to_all(
        blocks, "fsdp", split_axis=0, concat_axis=0, tiled=True, axis_index_groups=groups
    )


def on_device(
    tokens,
    positions,
    routes,
    cotangent,
    first_gain,
    w_query,
    w_key,
    w_value,
    w_out,
    second_gain,
    w_router,
    w_gate,
    w_up,
    w_down,
):
    width = tokens.shape[2]
    rows = tokens.shape[1]
    heads_all = w_query.shape[1] // HD
    kv_all = w_key.shape[1] // HD
    group = heads_all // kv_all
    q_width, kv_width = heads_all * HD, kv_all * HD
    scale = HD ** (-0.5)
    slots = lax.axis_size("fsdp")
    experts = slots // CORES
    seq = lax.axis_index("seq")
    places = BLOCK

    x_own = tokens[0]

    chosen = routes[0]
    ids = jnp.arange(experts, dtype=jnp.int32)
    mask = jnp.any(chosen[:, :, None] == ids[None, None, :], axis=1)
    mask_low = mask.astype(jnp.bfloat16)
    earlier = (jnp.arange(rows)[:, None] > jnp.arange(rows)[None, :]).astype(jnp.bfloat16)
    rank = jnp.where(mask, dot_plain(earlier, mask_low).astype(jnp.int32), -1)
    onehot_wide = rank.T[:, None, :] == jnp.arange(places, dtype=jnp.int32)[None, :, None]
    onehot = onehot_wide.astype(jnp.bfloat16).reshape(experts * places, rows)

    grad_low = cotangent[0]
    grad_output = grad_low.astype(jnp.float32)

    small = jnp.concatenate(
        [
            w_router,
            first_gain[:, None],
            second_gain[:, None],
            jnp.zeros((w_router.shape[0], SMALL - experts - 2), jnp.bfloat16),
        ],
        axis=1,
    )
    full_a, full_b, x_before, pos_before = gather_shards(
        jnp.concatenate([w_query, w_key], axis=1),
        jnp.concatenate([w_value, w_out, small], axis=1),
        x_own,
        positions,
    )
    query_full, key_full = full_a[:, :q_width], full_a[:, q_width:]
    value_full = full_b[:, :kv_width]
    out_full = full_b[:, kv_width : kv_width + width]
    small_full = full_b[:, kv_width + width :]
    router_full = small_full[:, :experts]
    gain_first = small_full[:, experts].astype(jnp.float32)
    gain_second = small_full[:, experts + 1].astype(jnp.float32)

    x_both = jnp.concatenate([x_before, x_own], axis=0).astype(jnp.float32)
    pos_both = jnp.concatenate([pos_before[0], positions[0]], axis=0)
    inputs = x_both[rows:]
    inverse = rope_base ** (-(2.0 * jnp.arange(HD // 2, dtype=jnp.float32)) / HD)
    angle = pos_both.astype(jnp.float32)[:, None] * inverse[None, :]
    cosine = jnp.cos(angle)[:, None, :]
    sine_table = jnp.sin(angle)[:, None, :]
    inverse_one = lax.rsqrt(jnp.mean(x_both * x_both, axis=-1, keepdims=True) + epsilon)
    normed_both = (x_both * inverse_one * gain_first).astype(jnp.bfloat16)
    normed_own = normed_both[rows:]
    query_pre = dot_plain(normed_own, query_full).reshape(rows, heads_all, HD)
    key_pre = dot_plain(normed_both, key_full).reshape(2 * rows, kv_all, HD)
    query_rot = (rotate(query_pre, cosine[rows:], sine_table[rows:]) * scale).astype(jnp.bfloat16)
    keyed = rotate(key_pre, cosine, sine_table).astype(jnp.bfloat16)
    valued = dot_plain(normed_both, value_full).astype(jnp.bfloat16).reshape(2 * rows, kv_all, HD)
    grouped = query_rot.reshape(rows, kv_all, group, HD)
    key_at = jnp.arange(2 * rows)[None, :]
    allowed = (key_at - rows <= jnp.arange(rows)[:, None]) & ((key_at >= rows) | (seq == 1))
    scores = jnp.einsum("qkgd,pkd->kgqp", grouped, keyed, preferred_element_type=jnp.float32)
    scores = jnp.where(allowed, scores, masked_score)
    peak = jnp.max(scores, axis=-1, keepdims=True)
    raised = jnp.exp(scores - peak)
    probs = raised / jnp.sum(raised, axis=-1, keepdims=True)
    probs_low = probs.astype(jnp.bfloat16)
    attended = (
        jnp.einsum("kgqp,pkd->qkgd", probs_low, valued, preferred_element_type=jnp.float32)
        .astype(jnp.bfloat16)
        .reshape(rows, q_width)
    )
    middle = inputs + dot_plain(attended, out_full)

    inverse_two = lax.rsqrt(jnp.mean(middle * middle, axis=-1, keepdims=True) + epsilon)
    normed_two = (middle * inverse_two * gain_second).astype(jnp.bfloat16)
    logits = jnp.where(mask, dot_plain(normed_two, router_full), masked_score)
    lifted = jnp.where(mask, jnp.exp(logits - jnp.max(logits, axis=-1, keepdims=True)), 0.0)
    gates = lifted / jnp.sum(lifted, axis=-1, keepdims=True)
    gates_wide = jnp.where(onehot_wide, gates.T[:, None, :], 0.0)
    gate_slots = jnp.sum(gates_wide, axis=-1, keepdims=True)
    gate_high, gate_rest = in_two(gate_slots)
    gates_sent = jnp.pad(
        jnp.concatenate([gate_high, gate_rest], axis=2), ((0, 0), (0, 0), (0, SMALL - 2))
    )

    part_out, grad_routed, dots, grad_gate, grad_up, grad_down = run_experts(
        onehot.reshape(experts, places, rows),
        gates_sent,
        normed_two,
        grad_low,
        w_gate[0],
        w_up[0],
        w_down[0],
    )
    returned = from_experts(part_out).reshape(experts * places, width)

    gates_high, gates_rest = in_two(gates_wide)
    flat = (experts * places, rows)
    mixed = dot_left(gates_high.reshape(flat), returned) + dot_left(
        gates_rest.reshape(flat), returned
    )
    layer_out = (middle + mixed).astype(jnp.bfloat16)
    dot_slots = dots[:, :, 0:1].astype(jnp.float32) + dots[:, :, 1:2].astype(jnp.float32)
    grad_gates = jnp.sum(jnp.where(onehot_wide, dot_slots, 0.0), axis=1).T
    grad_picked = gates * (grad_gates - jnp.sum(gates * grad_gates, axis=-1, keepdims=True))
    grad_logits = grad_picked.astype(jnp.bfloat16)
    grad_router = dot_left(normed_two, grad_logits)
    grad_normed_two = dot_right(grad_logits, router_full) + grad_routed

    normed = middle * inverse_two
    scaled = grad_normed_two * gain_second
    grad_middle = grad_output + inverse_two * (
        scaled - normed * jnp.mean(scaled * normed, axis=-1, keepdims=True)
    )
    grad_gain_second = jnp.sum(grad_normed_two * normed, axis=0)
    grad_branch = grad_middle.astype(jnp.bfloat16)
    grad_out_full = dot_left(attended, grad_branch).astype(jnp.bfloat16)
    grad_heads = (
        dot_right(grad_branch, out_full).astype(jnp.bfloat16).reshape(rows, kv_all, group, HD)
    )
    grad_probs = jnp.einsum(
        "qkgd,pkd->kgqp", grad_heads, valued, preferred_element_type=jnp.float32
    )
    grad_scores = (
        probs * (grad_probs - jnp.sum(probs * grad_probs, axis=-1, keepdims=True))
    ).astype(jnp.bfloat16)
    grad_value_in = (
        jnp.einsum("kgqp,qkgd->pkd", probs_low, grad_heads, preferred_element_type=jnp.float32)
        .astype(jnp.bfloat16)
        .reshape(2 * rows, kv_width)
    )
    grad_query_rot = (
        jnp.einsum("kgqp,pkd->qkgd", grad_scores, keyed, preferred_element_type=jnp.float32)
        .astype(jnp.bfloat16)
        .astype(jnp.float32)
        .reshape(rows, heads_all, HD)
    )
    grad_key_rot = (
        jnp.einsum("kgqp,qkgd->pkd", grad_scores, grouped, preferred_element_type=jnp.float32)
        .astype(jnp.bfloat16)
        .astype(jnp.float32)
    )
    grad_query_in = (
        (rotate(grad_query_rot, cosine[rows:], -sine_table[rows:]) * scale)
        .astype(jnp.bfloat16)
        .reshape(rows, q_width)
    )
    grad_key_in = (
        rotate(grad_key_rot, cosine, -sine_table).astype(jnp.bfloat16).reshape(2 * rows, kv_width)
    )
    grad_query_full = dot_left(normed_own, grad_query_in).astype(jnp.bfloat16)
    grad_key_full = dot_left(normed_both, grad_key_in).astype(jnp.bfloat16)
    grad_value_full = dot_left(normed_both, grad_value_in).astype(jnp.bfloat16)
    grad_both = dot_right(grad_key_in, key_full) + dot_right(grad_value_in, value_full)
    grad_before = grad_both[:rows].astype(jnp.bfloat16)
    grad_after = lax.ppermute(grad_before, "seq", [(1, 0)]).astype(jnp.float32)
    grad_own = grad_both[rows:] + dot_right(grad_query_in, query_full)
    normed_x = x_both * inverse_one
    grad_gain_first = jnp.sum(grad_own * normed_x[rows:], axis=0) + jnp.sum(
        grad_both[:rows] * normed_x[:rows], axis=0
    )
    small_grad = jnp.concatenate(
        [
            grad_router,
            grad_gain_first[:, None],
            grad_gain_second[:, None],
            jnp.zeros((width, SMALL - experts - 2), jnp.float32),
        ],
        axis=1,
    ).astype(jnp.bfloat16)
    scaled_one = (grad_own + grad_after) * gain_first
    grad_tokens = grad_middle + inverse_one[rows:] * (
        scaled_one
        - normed_x[rows:] * jnp.mean(scaled_one * normed_x[rows:], axis=-1, keepdims=True)
    )

    sum_out, sum_key, sum_query, sum_value, sum_small = scatter_sums(
        [grad_out_full, grad_key_full, grad_query_full, grad_value_full, small_grad],
        (0, 0, 1, 1, 1),
        1,
    )
    return (
        layer_out[None],
        grad_tokens[None],
        sum_small[:, experts],
        sum_query,
        sum_key,
        sum_value,
        sum_out,
        sum_small[:, experts + 1],
        sum_small[:, :experts],
        grad_gate[None],
        grad_up[None],
        grad_down[None],
    )


def solution(mesh):
    rows = P("fsdp", "seq", None)
    matrix, cube = P("fsdp", None), P("fsdp", None, None)
    return jax.shard_map(
        on_device,
        mesh=mesh,
        in_specs=(
            rows,
            P("fsdp", "seq"),
            rows,
            rows,
            P("fsdp"),
            matrix,
            matrix,
            matrix,
            matrix,
            P("fsdp"),
            matrix,
            cube,
            cube,
            cube,
        ),
        out_specs=(
            rows,
            rows,
            P("fsdp"),
            matrix,
            matrix,
            matrix,
            matrix,
            P("fsdp"),
            matrix,
            cube,
            cube,
            cube,
        ),
        check_vma=False,
    )
```

profile of v0, /device:TPU:1, one launch (start us, length us, event | category | flops | bytes accessed | tf_op | source)
XLA Modules:
  0.0 352.4 jit_solution(1469770488524998108)
XLA Ops:
  2.2 1.4 pad_maximum_fusion.1.shard_a
  3.6 1.5 concatenate.52.shard_b
  5.1 39.9 %gather_weights.1 = (bf16[2,4,4,2,16,1536]{5,4,3,2,1,0:T(8,128)(2,1)}, bf16[2,4,4,2,16,1664]{5,4,3,2,1,0:T(8,128)(2,1)}, bf16[128,1024]{1,0:T(8,128)(2,1)}, s32[1,128]{1,0:T(1,128)}) custom-call(bf16[16,1536]{1,0:T(8,128)(2,1)} %pad_maximum_fusion.1.shard_a, bf16[16,1664]{1,0:T(8,128)(2,1)} %concatenate.52.shard_b, bf16[128,1024]{1,0:T(8,128)(2,1)} %bitcast.169, ...), custom_call_target="tpu_custom_call" | custom-call | tf_op jit(solution)/shard_map/gather_weights/pallas_call | solution.py:221
  48.4 3.5 fusion.11
  51.9 1.7 fusion.37
  53.7 2.4 convolution_convert_fusion.6
  60.2 2.1 fusion.91
  62.3 2.0 convolution_convert_fusion.5
  69.7 173.0 %experts.1 = (bf16[32,48,1024]{2,1,0:T(8,128)(2,1)}, f32[128,1024]{1,0:T(8,128)}, bf16[32,48,128]{2,1,0:T(8,128)(2,1)}, f32[512,512]{1,0:T(8,128)}, f32[512,512]{1,0:T(8,128)}, /*index=5*/f32[256,1024]{1,0:T(8,128)}) custom-call(bf16[32,48,128]{2,1,0:T(8,128)(2,1)} %fusion.42.onehot, bf16[32,48,128]{2,1,0:T(8,128)(2,1)} %pad.4.gates, ...), custom_call_target="tpu_custom_call" | custom-call | tf_op jit(solution)/shard_map/experts/pallas_call | solution.py:745
  242.7 1.6 add_reduce_fusion
  244.7 2.3 multiply_reduce_fusion.1
  248.4 2.2 fusion.1
  253.1 1.7 fusion.35
  254.9 1.7 convolution_add_fusion
  258.8 6.6 %all-to-all-start = ((bf16[32,48,1024]{2,1,0:T(8,128)(2,1)}), bf16[32,48,1024]{2,1,0:T(8,128)(2,1)}, u32[]{:S(2)}, u32[]{:S(2)}) async-start(bf16[32,48,1024]{2,1,0:T(8,128)(2,1)} %get-tuple-element.31), calls=%async_computation | async-start | bytes 6291456 | tf_op jit(solution)/shard_map/all_to_all | solution.py:800
  269.2 1.5 convolution_convert_fusion.2
  270.7 2.1 convolution_convert_fusion
  273.8 1.5 convolution_convert_fusion.3
  275.4 2.7 multiply_reduce_fusion.2
  279.2 1.3 maximum_maximum_fusion.refs_4_
  281.8 56.1 %scatter_gradients.1 = (f32[16,1024]{1,0:T(8,128)S(1)}, f32[16,512]{1,0:T(8,128)S(1)}, f32[16,1024]{1,0:T(8,128)S(1)}, f32[16,512]{1,0:T(8,128)S(1)}, f32[16,128]{1,0:T(8,128)S(1)}) custom-call(bf16[2,4,4,2,16,1024]{5,4,3,2,1,0:T(8,128)(2,1)S(1)} %bitcast.157, bf16[2,4,4,2,16,512]{5,4,3,2,1,0:T(8,128)(2,1)S(1)} %bitcast.159, ...), custom_call_target="tpu_custom_call" | custom-call | tf_op jit(solution)/shard_map/scatter_gradients/pallas_call | solution.py:392
  338.6 1.9 add_bitcast_fusion
  340.6 2.6 convolution_bitcast_fusion.2
  343.1 3.3 fusion.30
  (183 shorter events, 34.3 us)
Async XLA Ops:
  0.6 45.8 %copy-start.12 = (bf16[1,128,1024]{2,1,0:T(8,128)(2,1)S(1)}, bf16[1,128,1024]{2,1,0:T(8,128)(2,1)}, u32[]{:S(2)}) copy-start(bf16[1,128,1024]{2,1,0:T(8,128)(2,1)} %param.14) | copy-start | bytes 786436
  46.5 5.5 %copy-start.43 = (f32[1024,1]{0,1:T(1,128)}, f32[1024,1]{0,1:T(1,128)S(1)}, u32[]{:S(2)}) copy-start(f32[1024,1]{0,1:T(1,128)S(1)} %copy.110) | copy-start | bytes 12292
  48.4 222.3 %copy-start.3 = (bf16[256,1024]{1,0:T(8,128)(2,1)}, bf16[256,1024]{1,0:T(8,128)(2,1)S(1)}, u32[]{:S(2)}) copy-start(bf16[256,1024]{1,0:T(8,128)(2,1)S(1)} %get-tuple-element.60) | copy-start | bytes 1572868
  57.1 5.2 %copy-start.37 = (f32[128,32]{0,1:T(8,128)}, f32[128,32]{0,1:T(8,128)S(1)}, u32[]{:S(2)}) copy-start(f32[128,32]{0,1:T(8,128)S(1)} %slice.137) | copy-start | bytes 49156
  57.8 4.5 %copy-start.27 = (bf16[256,8,32]{0,2,1:T(8,128)(2,1)}, bf16[256,8,32]{0,2,1:T(8,128)(2,1)S(1)}, u32[]{:S(2)}) copy-start(bf16[256,8,32]{0,2,1:T(8,128)(2,1)S(1)} %get-tuple-element.54) | copy-start | bytes 393220
  62.3 185.9 %copy-start.45 = (f32[8,2,128]{2,1,0:T(2,128)}, f32[8,2,128]{2,1,0:T(2,128)S(1)}, u32[]{:S(2)}) copy-start(f32[8,2,128]{2,1,0:T(2,128)S(1)} %get-tuple-element.68) | copy-start | bytes 24580
  65.5 181.5 %copy-start.1 = (f32[128,1024]{1,0:T(8,128)}, f32[128,1024]{1,0:T(8,128)S(1)}, u32[]{:S(2)}) copy-start(f32[128,1024]{1,0:T(8,128)S(1)} %get-tuple-element.71) | copy-start | bytes 1572868
  67.3 175.4 %copy-start.33 = (f32[32,128]{1,0:T(8,128)}, f32[32,128]{1,0:T(8,128)S(1)}, u32[]{:S(2)}) copy-start(f32[32,128]{1,0:T(8,128)S(1)} %fusion.75) | copy-start | bytes 49156
  242.7 4.3 %copy-start.23 = (bf16[1,128,1024]{2,1,0:T(8,128)(2,1)S(1)}, bf16[1,128,1024]{2,1,0:T(8,128)(2,1)}, u32[]{:S(2)}) copy-start(bf16[1,128,1024]{2,1,0:T(8,128)(2,1)} %param.17) | copy-start | bytes 786436
  257.4 17.9 %collective-permute-start = (bf16[128,1024]{1,0:T(8,128)(2,1)}, bf16[128,1024]{1,0:T(8,128)(2,1)}, u32[]{:S(2)}, u32[]{:S(2)}) collective-permute-start(bf16[128,1024]{1,0:T(8,128)(2,1)} %slice.214), channel_id=1, source_target_pairs={{64,0},{65,1},{66,2},{67,3},{68,4},{69,5},{70,6},{71,7},{72,8},{73... | collective-permute-start | bytes 786440 | tf_op jit(solution)/shard_map/ppermute | solution.py:983
  258.7 6.7 %copy-start.11 = (bf16[128,1024]{1,0:T(8,128)(2,1)S(1)}, bf16[128,1024]{1,0:T(8,128)(2,1)}, u32[]{:S(2)}) copy-start(bf16[128,1024]{1,0:T(8,128)(2,1)} %copy-done.10) | copy-start | bytes 786436
  258.7 6.7 %copy-start.41 = (bf16[128,32]{0,1:T(8,128)(2,1)S(1)}, bf16[128,32]{0,1:T(8,128)(2,1)}, u32[]{:S(2)}) copy-start(bf16[128,32]{0,1:T(8,128)(2,1)} %copy-done.40) | copy-start | bytes 24580
  258.7 6.9 %copy-start.49 = (f32[256]{0:T(256)S(1)}, f32[256]{0:T(256)}, u32[]{:S(2)}) copy-start(f32[256]{0:T(256)} %copy-done.48) | copy-start | bytes 3076
  258.8 8.2 %copy-start.47 = (bf16[1024]{0:T(1024)(128)(2,1)S(1)}, bf16[1024]{0:T(1024)(128)(2,1)}, u32[]{:S(2)}) copy-start(bf16[1024]{0:T(1024)(128)(2,1)} %get-tuple-element.44) | copy-start | bytes 6148
  258.8 9.9 %copy-start.28 = (bf16[256,8,32]{0,2,1:T(8,128)(2,1)S(1)}, bf16[256,8,32]{0,2,1:T(8,128)(2,1)}, u32[]{:S(2)}) copy-start(bf16[256,8,32]{0,2,1:T(8,128)(2,1)} %copy-done.27) | copy-start | bytes 393220
  258.8 81.8 %all-to-all-start = ((bf16[32,48,1024]{2,1,0:T(8,128)(2,1)}), bf16[32,48,1024]{2,1,0:T(8,128)(2,1)}, u32[]{:S(2)}, u32[]{:S(2)}) async-start(bf16[32,48,1024]{2,1,0:T(8,128)(2,1)} %get-tuple-element.31), calls=%async_computation | async-start | bytes 6291456 | tf_op jit(solution)/shard_map/all_to_all | solution.py:800
  270.7 4.6 %copy-start.32 = (bf16[2,4,4,2,16,1536]{5,4,3,2,1,0:T(8,128)(2,1)S(1)}, bf16[2,4,4,2,16,1536]{5,4,3,2,1,0:T(8,128)(2,1)}, u32[]{:S(2)}) copy-start(bf16[2,4,4,2,16,1536]{5,4,3,2,1,0:T(8,128)(2,1)} %get-tuple-element.29) | copy-start | bytes 9437188
  275.3 3.9 %copy-start.22 = (bf16[1024,32]{1,0:T(8,128)(2,1)S(1)}, bf16[1024,32]{1,0:T(8,128)(2,1)}, u32[]{:S(2)}) copy-start(bf16[1024,32]{1,0:T(8,128)(2,1)} %copy.95) | copy-start | bytes 196612
  281.7 56.9 %copy-start.9 = (f32[128,1024]{1,0:T(8,128)S(1)}, f32[128,1024]{1,0:T(8,128)}, u32[]{:S(2)}) copy-start(f32[128,1024]{1,0:T(8,128)} %copy-done.7) | copy-start | bytes 1572868
  281.7 56.9 %copy-start.14 = (f32[256,1024]{1,0:T(8,128)S(1)}, f32[256,1024]{1,0:T(8,128)}, u32[]{:S(2)}) copy-start(f32[256,1024]{1,0:T(8,128)} %get-tuple-element.59) | copy-start | bytes 3145732
  281.7 56.9 %copy-start.29 = (f32[128,1024]{1,0:T(8,128)S(1)}, f32[128,1024]{1,0:T(8,128)}, u32[]{:S(2)}) copy-start(f32[128,1024]{1,0:T(8,128)} %get-tuple-element.77) | copy-start | bytes 1572868
  281.7 56.9 %copy-start.52 = (f32[128]{0:T(128)S(1)}, f32[128]{0:T(128)}, u32[]{:S(2)}) copy-start(f32[128]{0:T(128)} %slice.116) | copy-start | bytes 1540
  343.1 6.4 %copy-start.21 = (f32[512,512]{1,0:T(8,128)S(1)}, f32[512,512]{1,0:T(8,128)}, u32[]{:S(2)}) copy-start(f32[512,512]{1,0:T(8,128)} %get-tuple-element.39) | copy-start | bytes 3145732
  346.4 4.1 %copy-start.20 = (f32[512,512]{1,0:T(8,128)S(1)}, f32[512,512]{1,0:T(8,128)}, u32[]{:S(2)}) copy-start(f32[512,512]{1,0:T(8,128)} %get-tuple-element.40) | copy-start | bytes 3145732
  (33 other events, 76.3 us)
where the time goes:
time: 353 us; the launch traced here: 352 us
  Pallas kernels  269 us (76%)
  matrix products  38.9 us (11%)
  local copies, waits for them, and re-layouts  20.8 us (6%)
  other arithmetic  14.3 us (4%)
  starting transfers between devices  7.91 us (2%)
    pallas_call x1, Pallas kernels, run_experts(): pl.pallas_call(expert_kernel, out_shape=[jax.ShapeDtypeStruct((chips, BLO...  173 us
    pallas_call x1, Pallas kernels, scatter_sums(): pl.pallas_call(functools.partial(scatter_kernel, groups), out_shape=[jax....  56.1 us
    pallas_call x1, Pallas kernels, gather_shards(): pl.pallas_call(gather_kernel, out_shape=outs, in_specs=[ANY] * 4, out_spe...  39.9 us
    dot_general x7, matrix products, dot_left(): lax.dot_general(left, right, (((0,), (0,)), ((), ())), preferred_element_...  11.7 us
    unnamed x120, local copies, waits for them, and re-layouts  9.67 us
    dot_general x6, matrix products, dot_plain(): return jnp.dot(left, right, preferred_element_type=jnp.float32)  9.6 us
    dot_general x5, matrix products, dot_right(): lax.dot_general(left, right, (((1,), (1,)), ((), ())), preferred_element_...  9.22 us
  transfers between devices with their start and end apart: 2, of which 0 were waited for; matrix products, arithmetic and copies ran while one was open for 5% of the time, Pallas kernels for 16%

commit v1 on v0

--- a/solution.py
+++ b/solution.py
@@ -248,13 +248,14 @@
     return values.astype(jnp.float32)
 
 
-def scatter_kernel(groups, *refs):
+def scatter_kernel(groups, before, *refs):
     number = len(groups)
+    after, refs = refs[2 * number], refs[: 2 * number] + refs[2 * number + 1 :]
     parts, totals = refs[:number], refs[number : 2 * number]
     halves, landed, second, landed_two, third, landed_three = (
         refs[k * number : (k + 1) * number] for k in range(2, 8)
     )
-    core_send, core_recv, send, recv = refs[8 * number :]
+    core_send, core_recv, send, recv, swap_sems = refs[8 * number :]
     seq, y, x, z, core = coordinates()
     far_y = [
         device(seq, 1 - y, x, z, core),
@@ -306,6 +307,15 @@
             )
             moved.start()
             across[i, j] = moved
+    swap = pltpu.make_async_remote_copy(
+        src_ref=before,
+        dst_ref=after,
+        send_sem=swap_sems.at[0],
+        recv_sem=swap_sems.at[1],
+        device_id=far_y[1],
+        device_id_type=MESH,
+    )
+    swap.start()
     for j in order:
         for i in range(number):
             across[i, j].wait_recv()
@@ -376,9 +386,10 @@
     for i in range(number):
         for j in order:
             across[i, j].wait_send()
-
-
-def scatter_sums(fulls, groups, identity):
+    swap.wait()
+
+
+def scatter_sums(fulls, groups, before, identity):
     count = lax.axis_size("fsdp")
     number = len(fulls)
     rows = fulls[0].shape[0] // count
@@ -391,9 +402,10 @@
 
     return pl.pallas_call(
         functools.partial(scatter_kernel, groups),
-        out_shape=[jax.ShapeDtypeStruct((rows, width), jnp.float32) for width in widths],
-        in_specs=[VMEM] * number,
-        out_specs=[VMEM] * number,
+        out_shape=[jax.ShapeDtypeStruct((rows, width), jnp.float32) for width in widths]
+        + [jax.ShapeDtypeStruct(before.shape, before.dtype)],
+        in_specs=[ANY] + [VMEM] * number,
+        out_specs=[VMEM] * number + [ANY],
         scratch_shapes=room(LONG, ys, LONG)
         + room(LONG - 1, ys, LONG)
         + room(ys, LONG)
@@ -405,32 +417,105 @@
             pltpu.SemaphoreType.DMA((number, LONG)),
             pltpu.SemaphoreType.DMA((number, 9)),
             pltpu.SemaphoreType.DMA((number, 9)),
+            pltpu.SemaphoreType.DMA((2,)),
         ],
         compiler_params=pltpu.CompilerParams(
             collective_id=identity, has_side_effects=True, vmem_limit_bytes=48 * 2**20
         ),
         name="scatter_gradients",
-    )(*parts)
+    )(before, *parts)
 
 
 CHUNKS = 4
 SAME, CROSS = 32, 16
 BLOCK = SAME + CROSS
-
-
-def chip_at(sign, step):
+PLANE = LONG * LONG
+
+
+def chip_at(sign, step, other_y=0):
     seq, y, x, z, core = coordinates()
-    chunk, inner = step // 8, step % 8
-    dy, dx = inner // LONG, inner % LONG
-    dz = (dx + chunk) % LONG
-    return ((y + dy) % 2 * LONG + (x + sign * dx + LONG) % LONG) * LONG + (
+    inner = step % PLANE
+    dx = inner % LONG
+    dz = (dx + inner // LONG) % LONG
+    return ((y + other_y) % 2 * LONG + (x + sign * dx + LONG) % LONG) * LONG + (
         z + sign * dz + LONG
     ) % LONG
 
 
+def remote(source, target, sends, recvs, to):
+    return pltpu.make_async_remote_copy(
+        src_ref=source,
+        dst_ref=target,
+        send_sem=sends,
+        recv_sem=recvs,
+        device_id=to,
+        device_id_type=MESH,
+    )
+
+
+class Rows:
+    def __init__(self, source, target, sems, self_sems, sign):
+        self.source, self.target, self.sems, self.self_sems = source, target, sems, self_sems
+        self.sign, self.steps = sign, 2 * PLANE // CHUNKS
+        self.depth = self.steps * BLOCK
+        self.seq, _, _, _, self.core = coordinates()
+        self.partner = (self.seq, lax.axis_index("fsdp") + 1 - 2 * self.core)
+
+    def rows(self, chunk):
+        return pl.ds(pl.multiple_of(chunk * self.depth, 16), self.depth)
+
+    def own(self, step):
+        rows = pl.ds(pl.multiple_of(step * BLOCK, 16), SAME)
+        return pltpu.make_async_copy(
+            self.source.at[rows], self.target.at[rows], self.self_sems.at[step // PLANE]
+        )
+
+    def send(self, chunk):
+        @pl.loop(0, self.steps)
+        def _(inner):
+            step = chunk * self.steps + inner
+            chip = chip_at(self.sign, step)
+            row = pl.multiple_of(step * BLOCK, 16)
+            same, cross = pl.ds(row, SAME), pl.ds(pl.multiple_of(row + SAME, 16), CROSS)
+
+            @pl.when(step % PLANE == 0)
+            def _():
+                self.own(step).start()
+
+            sems = (self.sems.at[0, chunk], self.sems.at[1, chunk])
+
+            @pl.when(step % PLANE > 0)
+            def _():
+                to = (self.seq, chip * CORES + self.core)
+                remote(self.source.at[same], self.target.at[same], *sems, to).start()
+
+            to = (self.seq, chip * CORES + 1 - self.core)
+            remote(self.source.at[cross], self.target.at[cross], *sems, to).start()
+
+    def whole(self, buffer, chunk, first):
+        rows = self.rows(chunk)
+        if first:
+            rows = pl.ds(pl.multiple_of(chunk * self.depth + SAME, 16), self.depth - SAME)
+        part = buffer.at[rows]
+        return remote(part, part, self.sems.at[0, chunk], self.sems.at[1, chunk], self.partner)
+
+    def wait(self, chunk):
+        @pl.when(chunk % 2 == 0)
+        def _():
+            self.own(chunk * self.steps).wait()
+            self.whole(self.target, chunk, True).wait_recv()
+
+        @pl.when(chunk % 2 == 1)
+        def _():
+            self.whole(self.target, chunk, False).wait_recv()
+
+    def wait_sends(self):
+        for chunk in range(CHUNKS):
+            self.whole(self.source, chunk, chunk % 2 == 0).wait_send()
+
+
 def expert_kernel(
-    onehot,
-    gates,
+    table,
     normed,
     grad_low,
     own_gate,
@@ -438,10 +523,12 @@
     own_down,
     out_ref,
     back_ref,
-    dots_ref,
     d_gate,
     d_up,
     d_down,
+    table_both,
+    normed_both,
+    grad_both,
     picks,
     x_send,
     g_send,
@@ -449,6 +536,8 @@
     g_land,
     out_rows,
     back_land,
+    back_sum,
+    back_sum_land,
     gate_pre,
     up_pre,
     hidden,
@@ -472,21 +561,20 @@
     out_sems,
     weight_sems,
     sum_sems,
+    near_sems,
 ):
     seq, y, x, z, core = coordinates()
     me = lax.axis_index("fsdp")
-    width = normed.shape[1]
-    chips = onehot.shape[0]
-    steps = chips // CHUNKS
-    depth = steps * BLOCK
+    rows_own, width = normed.shape
     partner = (seq, me + 1 - 2 * core)
     other_seq = (1 - seq, me)
+    other_y = device(seq, 1 - y, x, z, core)
 
     barrier = pltpu.get_barrier_semaphore()
-    for target in (partner, other_seq):
+    for target in (partner, other_seq, other_y):
         pl.semaphore_signal(barrier, inc=1, device_id=target, device_id_type=MESH)
 
-    @pl.loop(1, chips)
+    @pl.loop(1, PLANE)
     def _(step):
         for side in range(CORES):
             pl.semaphore_signal(
@@ -496,17 +584,18 @@
                 device_id_type=MESH,
             )
 
-    pl.semaphore_wait(barrier, CORES * chips)
-
-    def remote(source, target, sends, recvs, to):
-        return pltpu.make_async_remote_copy(
-            src_ref=source,
-            dst_ref=target,
-            send_sem=sends,
-            recv_sem=recvs,
-            device_id=to,
-            device_id_type=MESH,
+    pl.semaphore_wait(barrier, CORES * PLANE + 1)
+
+    mine = pl.ds(pl.multiple_of(y * PLANE, PLANE), PLANE)
+    theirs = pl.ds(pl.multiple_of((1 - y) * PLANE, PLANE), PLANE)
+    near = [
+        remote(source, target.at[1], near_sems.at[0, i], near_sems.at[1, i], other_y)
+        for i, (source, target) in enumerate(
+            ((table.at[theirs], table_both), (normed, normed_both), (grad_low, grad_both))
         )
+    ]
+    for moved in near:
+        moved.start()
 
     weights = []
     for i, (own, full) in enumerate(((own_gate, w_gate), (own_up, w_up), (own_down, w_down))):
@@ -518,75 +607,58 @@
         sent.start()
         weights.append((kept, sent))
 
-    def send_block(source, target, sems, kind, sign, step):
-        chip = chip_at(sign, step)
-        chunk = step // steps
-        row = pl.multiple_of(step * BLOCK, 16)
-        same, cross = pl.ds(row, SAME), pl.ds(pl.multiple_of(row + SAME, 16), CROSS)
-
-        @pl.when(step == 0)
-        def _():
-            pltpu.make_async_copy(source.at[same], target.at[same], self_sems.at[kind]).start()
-
-        @pl.when(step > 0)
-        def _():
-            remote(
-                source.at[same],
-                target.at[same],
-                sems.at[0, chunk],
-                sems.at[1, chunk],
-                (seq, chip * CORES + core),
-            ).start()
-
-        remote(
-            source.at[cross],
-            target.at[cross],
-            sems.at[0, chunk],
-            sems.at[1, chunk],
-            (seq, chip * CORES + 1 - core),
-        ).start()
-
-    def whole(buffer, sems, chunk, first):
-        rows = pl.ds(SAME, depth - SAME) if first else pl.ds(pl.multiple_of(chunk * depth, 16), depth)
-        part = buffer.at[rows]
-        return remote(part, part, sems.at[0, chunk], sems.at[1, chunk], partner)
-
-    def wait_chunk(source, target, sems, kind, chunk):
-        @pl.when(chunk == 0)
-        def _():
-            pltpu.make_async_copy(
-                source.at[pl.ds(0, SAME)], target.at[pl.ds(0, SAME)], self_sems.at[kind]
-            ).wait()
-            whole(target, sems, 0, True).wait_recv()
-
-        @pl.when(chunk > 0)
-        def _():
-            whole(target, sems, chunk, False).wait_recv()
-
-    def wait_sends(source, sems):
-        for chunk in range(CHUNKS):
-            whole(source, sems, chunk, chunk == 0).wait_send()
-
-    @pl.loop(0, chips)
-    def _(step):
-        chip = chip_at(1, step)
-        rows = pl.ds(pl.multiple_of(step * BLOCK, 16), BLOCK)
-        picks[rows, :] = onehot[chip]
-        x_send[rows, width:] = gates[chip]
-
-    for values, buffer, target, sems, kind in (
-        (normed, x_send, x_land, x_sems, 0),
-        (grad_low, g_send, g_land, g_sems, 1),
-    ):
-
-        @pl.loop(0, CHUNKS)
-        def _(chunk):
-            rows = pl.ds(pl.multiple_of(chunk * depth, 16), depth)
-            buffer[rows, :width] = dot_plain(picks[rows, :], values[...]).astype(jnp.bfloat16)
-
-            @pl.loop(0, steps)
-            def _(inner):
-                send_block(buffer, target, sems, kind, 1, chunk * steps + inner)
+    x_rows = Rows(x_send.at[:, pl.ds(0, width)], x_land, x_sems, self_sems.at[0], 1)
+    g_rows = Rows(g_send, g_land, g_sems, self_sems.at[1], 1)
+    back_rows = Rows(x_send, back_land, back_sems, self_sems.at[2], -1)
+    steps, depth = x_rows.steps, x_rows.depth
+
+    table_both[0] = table[mine]
+    normed_both[0] = normed[...]
+    grad_both[0] = grad_low[...]
+    place = lax.broadcasted_iota(jnp.int32, (BLOCK, rows_own), 0).astype(jnp.float32)
+
+    def entry(step):
+        return table_both[step // PLANE, chip_at(1, step) % PLANE]
+
+    def send_x(chunk):
+        @pl.loop(0, steps)
+        def _(inner):
+            step = chunk * steps + inner
+            found = jnp.where(entry(step)[0:1] == place, 1.0, 0.0)
+            picks[pl.ds(pl.multiple_of(step * BLOCK, 16), BLOCK), :] = found.astype(jnp.bfloat16)
+
+        rows = x_rows.rows(chunk)
+        values = dot_plain(picks[rows, :], normed_both[chunk // 2])
+        x_send[rows, :width] = values.astype(jnp.bfloat16)
+        x_rows.send(chunk)
+
+    def send_g(chunk):
+        @pl.loop(0, steps)
+        def _(inner):
+            step = chunk * steps + inner
+            line = entry(step)
+            weight = jnp.where(line[0:1] == place, line[1:2], 0.0)
+            high = weight.astype(jnp.bfloat16)
+            rest = (weight - high.astype(jnp.float32)).astype(jnp.bfloat16)
+            rows = pl.ds(pl.multiple_of(step * BLOCK, 16), BLOCK)
+            values = dot_plain(high, grad_both[step // PLANE]) + dot_plain(
+                rest, grad_both[step // PLANE]
+            )
+            g_send[rows, :] = values.astype(jnp.bfloat16)
+
+        g_rows.send(chunk)
+
+    for chunk in (0, 1):
+        send_x(chunk)
+    near[0].wait_recv()
+    near[1].wait_recv()
+    for chunk in (2, 3):
+        send_x(chunk)
+    near[2].wait_recv()
+
+    @pl.loop(0, CHUNKS)
+    def _(turn):
+        send_g((turn + 2) % CHUNKS)
 
     for kept, sent in weights:
         kept.wait()
@@ -594,9 +666,9 @@
 
     @pl.loop(0, CHUNKS)
     def _(chunk):
-        rows = pl.ds(pl.multiple_of(chunk * depth, 16), depth)
-        wait_chunk(x_send, x_land, x_sems, 0, chunk)
-        served = x_land[rows, :width]
+        rows = x_rows.rows(chunk)
+        x_rows.wait(chunk)
+        served = x_land[rows, :]
         gate = dot_plain(served, w_gate[...])
         up = dot_plain(served, w_up[...])
         gate_pre[rows, :] = gate
@@ -609,7 +681,7 @@
         def _(inner):
             step = chunk * steps + inner
             row = pl.multiple_of(step * BLOCK, 16)
-            chip = chip_at(-1, step)
+            chip = chip_at(-1, step, step // PLANE)
             out_ref[chip, :SAME, :] = out_rows[pl.ds(row, SAME), :]
             remote(
                 out_rows.at[pl.ds(pl.multiple_of(row + SAME, 16), CROSS)],
@@ -619,22 +691,24 @@
                 partner,
             ).start()
 
-    wait_sends(x_send, x_sems)
+    x_rows.wait_sends()
+
+    lane = lax.broadcasted_iota(jnp.int32, (depth, SMALL), 1)
+    expert = me // CORES
 
     @pl.loop(0, CHUNKS)
-    def _(chunk):
-        rows = pl.ds(pl.multiple_of(chunk * depth, 16), depth)
-        wait_chunk(g_send, g_land, g_sems, 1, chunk)
-        grads = g_land[rows, :].astype(jnp.float32)
-        dots = jnp.sum(grads * out_rows[rows, :].astype(jnp.float32), axis=1, keepdims=True)
+    def _(turn):
+        chunk = (turn + 2) % CHUNKS
+        rows = g_rows.rows(chunk)
+        g_rows.wait(chunk)
+        low = g_land[rows, :]
+        dots = jnp.sum(
+            low.astype(jnp.float32) * out_rows[rows, :].astype(jnp.float32), axis=1, keepdims=True
+        )
         high = dots.astype(jnp.bfloat16).astype(jnp.float32)
-        lane = lax.broadcasted_iota(jnp.int32, (depth, SMALL), 1)
         x_send[rows, width:] = jnp.where(
-            lane == 0, high, jnp.where(lane == 1, dots - high, 0.0)
+            lane == expert, high, jnp.where(lane == expert + 2 * PLANE, dots - high, 0.0)
         ).astype(jnp.bfloat16)
-        weight = jnp.sum(x_land[rows, width:].astype(jnp.float32), axis=1, keepdims=True)
-        low = (weight * grads).astype(jnp.bfloat16)
-        g_land[rows, :] = low
         d_hidden = dot_right(low, w_down[...])
         gate, up = gate_pre[rows, :], up_pre[rows, :]
         sigmoid = jax.nn.sigmoid(gate)
@@ -645,10 +719,7 @@
         x_send[rows, :width] = (dot_right(one, w_gate[...]) + dot_right(two, w_up[...])).astype(
             jnp.bfloat16
         )
-
-        @pl.loop(0, steps)
-        def _(inner):
-            send_block(x_send, back_land, back_sems, 2, -1, chunk * steps + inner)
+        back_rows.send(chunk)
 
     tile = 256
     half = own_gate.shape[0]
@@ -696,8 +767,10 @@
         d_down[:, columns] = values
 
     pairs[0].wait_recv()
-    for which, mine in enumerate((d_gate, d_up)):
-        seq_send[which] = (mine[...] + pair_land[which].astype(jnp.float32)).astype(jnp.bfloat16)
+    for which, mine_sum in enumerate((d_gate, d_up)):
+        seq_send[which] = (mine_sum[...] + pair_land[which].astype(jnp.float32)).astype(
+            jnp.bfloat16
+        )
     pairs[1].wait_recv()
     seq_send_down[...] = (d_down[...] + pair_land_down[...].astype(jnp.float32)).astype(
         jnp.bfloat16
@@ -711,33 +784,44 @@
 
     back_ref[...] = jnp.zeros_like(back_ref)
 
-    @pl.loop(0, CHUNKS)
+    def combine(chunk):
+        rows = back_rows.rows(chunk)
+        back_rows.wait(chunk)
+        back_ref[...] += dot_left(picks[rows, :], back_land[rows, :])
+
+    @pl.loop(2, CHUNKS)
     def _(chunk):
-        rows = pl.ds(pl.multiple_of(chunk * depth, 16), depth)
-        wait_chunk(x_send, back_land, back_sems, 2, chunk)
-        back_ref[...] += dot_left(picks[rows, :], back_land[rows, :width])
-
-    @pl.loop(0, chips)
-    def _(step):
-        rows = pl.ds(pl.multiple_of(step * BLOCK, 16), BLOCK)
-        dots_ref[chip_at(1, step)] = back_land[rows, width:]
+        combine(chunk)
+
+    back_sum[...] = back_ref[...].astype(jnp.bfloat16)
+    over = remote(back_sum, back_sum_land, near_sems.at[0, 3], near_sems.at[1, 3], other_y)
+    over.start()
+    back_ref[...] = jnp.zeros_like(back_ref)
+
+    @pl.loop(0, 2)
+    def _(chunk):
+        combine(chunk)
+
+    over.wait_recv()
+    back_ref[...] += back_sum_land[...].astype(jnp.float32)
 
     sums[0].wait_recv()
-    for which, mine in enumerate((d_gate, d_up)):
-        mine[...] = seq_send[which].astype(jnp.float32) + seq_land[which].astype(jnp.float32)
+    for which, mine_sum in enumerate((d_gate, d_up)):
+        mine_sum[...] = seq_send[which].astype(jnp.float32) + seq_land[which].astype(jnp.float32)
     sums[1].wait_recv()
     d_down[...] = seq_send_down[...].astype(jnp.float32) + seq_land_down[...].astype(jnp.float32)
-    outs = out_rows.at[pl.ds(0, chips * CROSS)]
+    outs = out_rows.at[pl.ds(0, 2 * PLANE * CROSS)]
     remote(outs, outs, out_sems.at[0], out_sems.at[1], partner).wait()
-    wait_sends(g_send, g_sems)
-    wait_sends(x_send, back_sems)
-    for moved in pairs + sums:
+    g_rows.wait_sends()
+    back_rows.wait_sends()
+    for moved in pairs + sums + near + [over]:
         moved.wait_send()
 
 
-def run_experts(onehot, gates, normed, grad_low, own_gate, own_up, own_down):
-    chips, _, rows = onehot.shape
-    width, hidden = normed.shape[1], own_gate.shape[1]
+def run_experts(table, normed, grad_low, own_gate, own_up, own_down):
+    chips = table.shape[0]
+    rows, width = normed.shape
+    hidden = own_gate.shape[1]
     slots = chips * BLOCK
     low, high = jnp.bfloat16, jnp.float32
     dma = pltpu.SemaphoreType.DMA
@@ -746,22 +830,26 @@
         expert_kernel,
         out_shape=[
             jax.ShapeDtypeStruct((chips, BLOCK, width), low),
-            jax.ShapeDtypeStruct((rows, width), high),
-            jax.ShapeDtypeStruct((chips, BLOCK, SMALL), low),
+            jax.ShapeDtypeStruct((rows, width + SMALL), high),
             jax.ShapeDtypeStruct(own_gate.shape, high),
             jax.ShapeDtypeStruct(own_up.shape, high),
             jax.ShapeDtypeStruct(own_down.shape, high),
         ],
-        in_specs=[VMEM] * 7,
-        out_specs=[VMEM] * 6,
+        in_specs=[VMEM] * 6,
+        out_specs=[VMEM] * 5,
         scratch_shapes=[
+            pltpu.VMEM((2, PLANE, *table.shape[1:]), high),
+            pltpu.VMEM((2, rows, width), low),
+            pltpu.VMEM((2, rows, width), low),
             pltpu.VMEM((slots, rows), low),
             pltpu.VMEM((slots, width + SMALL), low),
             pltpu.VMEM((slots, width), low),
-            pltpu.VMEM((slots, width + SMALL), low),
+            pltpu.VMEM((slots, width), low),
             pltpu.VMEM((slots, width), low),
             pltpu.VMEM((slots, width), low),
             pltpu.VMEM((slots, width + SMALL), low),
+            pltpu.VMEM((rows, width + SMALL), low),
+            pltpu.VMEM((rows, width + SMALL), low),
             pltpu.VMEM((slots, hidden), high),
             pltpu.VMEM((slots, hidden), high),
             pltpu.VMEM((slots, hidden), low),
@@ -781,16 +869,17 @@
             dma((2, CHUNKS)),
             dma((2, CHUNKS)),
             dma((2, CHUNKS)),
-            dma((3,)),
+            dma((3, 2)),
             dma((2,)),
             dma((3, 3)),
+            dma((2, 4)),
             dma((2, 4)),
         ],
         compiler_params=pltpu.CompilerParams(
             collective_id=2, has_side_effects=True, vmem_limit_bytes=60 * 2**20
         ),
         name="experts",
-    )(onehot, gates, normed, grad_low, own_gate, own_up, own_down)
+    )(table, normed, grad_low, own_gate, own_up, own_down)
 
 
 def from_experts(blocks):
@@ -839,8 +928,6 @@
     earlier = (jnp.arange(rows)[:, None] > jnp.arange(rows)[None, :]).astype(jnp.bfloat16)
     rank = jnp.where(mask, dot_plain(earlier, mask_low).astype(jnp.int32), -1)
     onehot_wide = rank.T[:, None, :] == jnp.arange(places, dtype=jnp.int32)[None, :, None]
-    onehot = onehot_wide.astype(jnp.bfloat16).reshape(experts * places, rows)
-
     grad_low = cotangent[0]
     grad_output = grad_low.astype(jnp.float32)
 
@@ -903,33 +990,22 @@
     logits = jnp.where(mask, dot_plain(normed_two, router_full), masked_score)
     lifted = jnp.where(mask, jnp.exp(logits - jnp.max(logits, axis=-1, keepdims=True)), 0.0)
     gates = lifted / jnp.sum(lifted, axis=-1, keepdims=True)
+    table = jnp.stack([rank.T.astype(jnp.float32), gates.T], axis=1)
+    part_out, grad_back, grad_gate, grad_up, grad_down = run_experts(
+        table, normed_two, grad_low, w_gate[0], w_up[0], w_down[0]
+    )
+    grad_routed, dots = grad_back[:, :width], grad_back[:, width:]
+    returned = from_experts(part_out).reshape(experts * places, width)
+
     gates_wide = jnp.where(onehot_wide, gates.T[:, None, :], 0.0)
-    gate_slots = jnp.sum(gates_wide, axis=-1, keepdims=True)
-    gate_high, gate_rest = in_two(gate_slots)
-    gates_sent = jnp.pad(
-        jnp.concatenate([gate_high, gate_rest], axis=2), ((0, 0), (0, 0), (0, SMALL - 2))
-    )
-
-    part_out, grad_routed, dots, grad_gate, grad_up, grad_down = run_experts(
-        onehot.reshape(experts, places, rows),
-        gates_sent,
-        normed_two,
-        grad_low,
-        w_gate[0],
-        w_up[0],
-        w_down[0],
-    )
-    returned = from_experts(part_out).reshape(experts * places, width)
-
     gates_high, gates_rest = in_two(gates_wide)
     flat = (experts * places, rows)
     mixed = dot_left(gates_high.reshape(flat), returned) + dot_left(
         gates_rest.reshape(flat), returned
     )
     layer_out = (middle + mixed).astype(jnp.bfloat16)
-    dot_slots = dots[:, :, 0:1].astype(jnp.float32) + dots[:, :, 1:2].astype(jnp.float32)
-    grad_gates = jnp.sum(jnp.where(onehot_wide, dot_slots, 0.0), axis=1).T
-    grad_picked = gates * (grad_gates - jnp.sum(gates * grad_gates, axis=-1, keepdims=True))
+    weighted = dots[:, :experts] + dots[:, experts : 2 * experts]
+    grad_picked = weighted - gates * jnp.sum(weighted, axis=-1, keepdims=True)
     grad_logits = grad_picked.astype(jnp.bfloat16)
     grad_router = dot_left(normed_two, grad_logits)
     grad_normed_two = dot_right(grad_logits, router_full) + grad_routed
@@ -980,7 +1056,6 @@
     grad_value_full = dot_left(normed_both, grad_value_in).astype(jnp.bfloat16)
     grad_both = dot_right(grad_key_in, key_full) + dot_right(grad_value_in, value_full)
     grad_before = grad_both[:rows].astype(jnp.bfloat16)
-    grad_after = lax.ppermute(grad_before, "seq", [(1, 0)]).astype(jnp.float32)
     grad_own = grad_both[rows:] + dot_right(grad_query_in, query_full)
     normed_x = x_both * inverse_one
     grad_gain_first = jnp.sum(grad_own * normed_x[rows:], axis=0) + jnp.sum(
@@ -995,16 +1070,16 @@
         ],
         axis=1,
     ).astype(jnp.bfloat16)
-    scaled_one = (grad_own + grad_after) * gain_first
+    sum_out, sum_key, sum_query, sum_value, sum_small, grad_after = scatter_sums(
+        [grad_out_full, grad_key_full, grad_query_full, grad_value_full, small_grad],
+        (0, 0, 1, 1, 1),
+        grad_before,
+        1,
+    )
+    scaled_one = (grad_own + grad_after.astype(jnp.float32)) * gain_first
     grad_tokens = grad_middle + inverse_one[rows:] * (
         scaled_one
         - normed_x[rows:] * jnp.mean(scaled_one * normed_x[rows:], axis=-1, keepdims=True)
-    )
-
-    sum_out, sum_key, sum_query, sum_value, sum_small = scatter_sums(
-        [grad_out_full, grad_key_full, grad_query_full, grad_value_full, small_grad],
-        (0, 0, 1, 1, 1),
-        1,
     )
     return (
         layer_out[None],

time: 353 us -> 299 us (0.85)
  Pallas kernels: 269 us -> 221 us
  matrix products: 38.9 us -> 35.1 us
    pallas_call x1, Pallas kernels: 173 us -> 139 us  [run_experts(): pl.pallas_call(expert_kernel, out_shape=[jax.ShapeDtypeStruct((chips, BLO...]
    pallas_call x1, Pallas kernels: 56.1 us -> 41.5 us  [scatter_sums(): pl.pallas_call(functools.partial(scatter_kernel, groups), out_shape=[jax....]
    unnamed x120 -> x94, local copies, waits for them, and re-layouts: 9.67 us -> 8.44 us
  transfers between devices with their start and end apart: 2 -> 1, of which waited for: 0 -> 0; matrix products, arithmetic and copies ran while one was open for 5% -> 10% of each run, Pallas kernels for 16% -> 14%
where the time goes in v1:
time: 299 us; the launch traced here: 298 us
  Pallas kernels  221 us (74%)
  matrix products  35.1 us (12%)
  local copies, waits for them, and re-layouts  19.6 us (7%)
  other arithmetic  16.1 us (5%)
  starting transfers between devices  5.18 us (2%)
    pallas_call x1, Pallas kernels, run_experts(): pl.pallas_call(expert_kernel, out_shape=[jax.ShapeDtypeStruct((chips, BLO...  139 us
    pallas_call x1, Pallas kernels, scatter_sums(): pl.pallas_call(functools.partial(scatter_kernel, groups), out_shape=[jax....  41.5 us
    pallas_call x1, Pallas kernels, gather_shards(): pl.pallas_call(gather_kernel, out_shape=outs, in_specs=[ANY] * 4, out_spe...  39.9 us
    dot_general x7, matrix products, dot_left(): lax.dot_general(left, right, (((0,), (0,)), ((), ())), preferred_element_...  11.3 us
    unnamed x94, local copies, waits for them, and re-layouts  8.44 us
    dot_general x5, matrix products, dot_right(): lax.dot_general(left, right, (((1,), (1,)), ((), ())), preferred_element_...  8.11 us
    dot_general x6, matrix products, dot_plain(): return jnp.dot(left, right, preferred_element_type=jnp.float32)  7.16 us
  transfers between devices with their start and end apart: 1, of which 0 were waited for; matrix products, arithmetic and copies ran while one was open for 10% of the time, Pallas kernels for 14%

profile of v1, /device:TPU:1, one launch (start us, length us, event | category | flops | bytes accessed | tf_op | source)
XLA Modules:
  0.0 298.0 jit_solution(324435633176292580)
XLA Ops:
  3.8 1.4 pad_maximum_fusion.1.shard_a
  5.2 1.5 concatenate.49.shard_b
  6.6 39.9 %gather_weights.1 = (bf16[2,4,4,2,16,1536]{5,4,3,2,1,0:T(8,128)(2,1)}, bf16[2,4,4,2,16,1664]{5,4,3,2,1,0:T(8,128)(2,1)}, bf16[128,1024]{1,0:T(8,128)(2,1)}, s32[1,128]{1,0:T(1,128)}) custom-call(bf16[16,1536]{1,0:T(8,128)(2,1)} %pad_maximum_fusion.1.shard_a, bf16[16,1664]{1,0:T(8,128)(2,1)} %concatenate.49.shard_b, bf16[128,1024]{1,0:T(8,128)(2,1)} %bitcast.161, ...), custom_call_target="tpu_custom_call" | custom-call | tf_op jit(solution)/shard_map/gather_weights/pallas_call | solution.py:221
  49.0 2.1 slice_convert_fusion.1
  51.5 2.5 convolution_convert_fusion.6
  54.0 1.7 fusion.11
  58.8 1.8 copy.72
  63.0 2.1 fusion.84
  65.1 2.1 convolution_convert_fusion.5
  69.8 139.3 %experts.1 = (bf16[32,48,1024]{2,1,0:T(8,128)(2,1)}, f32[128,1152]{1,0:T(8,128)}, f32[512,512]{1,0:T(8,128)}, f32[512,512]{1,0:T(8,128)}, f32[256,1024]{1,0:T(8,128)}) custom-call(f32[32,2,128]{2,1,0:T(2,128)} %pad_maximum_fusion.2.table, bf16[128,1024]{1,0:T(8,128)(2,1)} %copy-done.3, bf16[128,1024]{1,0:T(8,128)(2,1)} %bitcast.174, ...), custom_call_target="tpu_custom_call" | custom-call | tf_op jit(solution)/shard_map/experts/pallas_call | solution.py:829
  209.2 5.2 %all-to-all-start = ((bf16[32,48,1024]{2,1,0:T(8,128)(2,1)}), bf16[32,48,1024]{2,1,0:T(8,128)(2,1)}, u32[]{:S(2)}, u32[]{:S(2)}) async-start(bf16[32,48,1024]{2,1,0:T(8,128)(2,1)} %get-tuple-element.31), calls=%async_computation | async-start | bytes 6291456 | tf_op jit(solution)/shard_map/all_to_all | solution.py:889
  216.1 2.1 multiply_reduce_fusion.2
  219.4 2.2 fusion.23
  225.2 1.7 copy.85
  226.9 1.8 concatenate.63
  229.6 1.7 fusion.34
  231.4 1.9 convolution_add_fusion
  233.8 1.6 fusion.41
  236.7 1.4 maximum_maximum_fusion.refs_4_
  238.0 1.4 convolution_convert_fusion.2
  240.0 2.1 convolution_convert_fusion
  242.8 41.5 %scatter_gradients.1 = (f32[16,1024]{1,0:T(8,128)S(1)}, f32[16,512]{1,0:T(8,128)S(1)}, f32[16,1024]{1,0:T(8,128)S(1)}, f32[16,512]{1,0:T(8,128)S(1)}, f32[16,128...) custom-call(bf16[128,1024]{1,0:T(8,128)(2,1)S(1)} %slice.230.before, bf16[2,4,4,2,16,1024]{5,4,3,2,1,0:T(8,128)(2,1)S(1)} %bitcast.149, ...), custom_call_target="tpu_custom_call" | custom-call | tf_op jit(solution)/shard_map/scatter_gradients/pallas_call | solution.py:403
  286.2 2.5 convolution_bitcast_fusion.2
  288.7 3.3 %fusion.30 = bf16[1,128,1024]{2,1,0:T(8,128)(2,1)} fusion(f32[128,1024]{1,0:T(8,128)S(1)} %get-tuple-element.68, f32[128,1024]{1,0:T(8,128)S(1)} %convolution_bitcast_fusion.2, bf16[32,48,1024]{2,1,0:T(8,128)(2,1)} %all-to-all-done, f32[32,128]{1,0:T(8,128)S(1)} %fusion.71, s32[32,128]{1,0:T(8,128)S(1)} %copy-done.28), kind=kOutput, calls=%fused_computation.41 | convolution fusion | flops 403832832 | bytes 4489216 | tf_op jit(solution)/shard_map/dot_general | solution.py:27
  (152 shorter events, 31.8 us)
Async XLA Ops:
  46.6 4.7 %copy-start.2 = (bf16[1,128,1024]{2,1,0:T(8,128)(2,1)S(1)}, bf16[1,128,1024]{2,1,0:T(8,128)(2,1)}, u32[]{:S(2)}) copy-start(bf16[1,128,1024]{2,1,0:T(8,128)(2,1)} %param.14) | copy-start | bytes 786436
  46.6 4.7 %copy-start.5 = (bf16[128,1024]{1,0:T(8,128)(2,1)S(1)}, bf16[128,1024]{1,0:T(8,128)(2,1)}, u32[]{:S(2)}) copy-start(bf16[128,1024]{1,0:T(8,128)(2,1)} %get-tuple-element.27) | copy-start | bytes 786436
  51.3 2.8 copy-start.31
  51.3 2.7 copy-start.25
  54.0 3.1 %copy-start.39 = (s32[1,128]{1,0:T(1,128)S(1)}, s32[1,128]{1,0:T(1,128)}, u32[]{:S(2)}) copy-start(s32[1,128]{1,0:T(1,128)} %pos_own.1) | copy-start | bytes 1540
  54.0 3.1 %copy-start.41 = (s32[1,128]{1,0:T(1,128)S(1)}, s32[1,128]{1,0:T(1,128)}, u32[]{:S(2)}) copy-start(s32[1,128]{1,0:T(1,128)} %get-tuple-element.30) | copy-start | bytes 1540
  54.0 4.6 %copy-start.6 = (f32[1024,1]{1,0:T(8,128)S(1)}, f32[1024,1]{1,0:T(8,128)}, u32[]{:S(2)}) copy-start(f32[1024,1]{1,0:T(8,128)} %get-tuple-element.48) | copy-start | bytes 12292
  58.0 7.1 %copy-start.24 = (f32[256,32]{0,1:T(8,128)}, f32[256,32]{0,1:T(8,128)S(1)}, u32[]{:S(2)}) copy-start(f32[256,32]{0,1:T(8,128)S(1)} %get-tuple-element.64) | copy-start | bytes 98308
  58.0 7.1 %copy-start.29 = (f32[128,32]{0,1:T(8,128)}, f32[128,32]{0,1:T(8,128)S(1)}, u32[]{:S(2)}) copy-start(f32[128,32]{0,1:T(8,128)S(1)} %slice.144) | copy-start | bytes 49156
  61.7 3.4 %copy-start.22 = (bf16[256,8,32]{0,2,1:T(8,128)(2,1)}, bf16[256,8,32]{0,2,1:T(8,128)(2,1)S(1)}, u32[]{:S(2)}) copy-start(bf16[256,8,32]{0,2,1:T(8,128)(2,1)S(1)} %get-tuple-element.53) | copy-start | bytes 393220
  63.0 4.3 %copy-start.18 = (f32[128,16,32]{0,2,1:T(8,128)}, f32[128,16,32]{0,2,1:T(8,128)S(1)}, u32[]{:S(2)}) copy-start(f32[128,16,32]{0,2,1:T(8,128)S(1)} %get-tuple-element.56) | copy-start | bytes 786436
  63.0 4.3 %copy-start.20 = (f32[128,16,32]{0,2,1:T(8,128)}, f32[128,16,32]{0,2,1:T(8,128)S(1)}, u32[]{:S(2)}) copy-start(f32[128,16,32]{0,2,1:T(8,128)S(1)} %get-tuple-element.57) | copy-start | bytes 786436
  209.2 5.2 %copy-start.38 = (f32[256]{0:T(256)S(1)}, f32[256]{0:T(256)}, u32[]{:S(2)}) copy-start(f32[256]{0:T(256)} %copy-done.37) | copy-start | bytes 3076
  209.2 5.8 %copy-start.13 = (f32[128,1152]{1,0:T(8,128)S(1)}, f32[128,1152]{1,0:T(8,128)}, u32[]{:S(2)}) copy-start(f32[128,1152]{1,0:T(8,128)} %get-tuple-element.32) | copy-start | bytes 1769476
  209.2 6.1 %copy-start.4 = (bf16[128,1024]{1,0:T(8,128)(2,1)S(1)}, bf16[128,1024]{1,0:T(8,128)(2,1)}, u32[]{:S(2)}) copy-start(bf16[128,1024]{1,0:T(8,128)(2,1)} %copy-done.3) | copy-start | bytes 786436
  209.2 77.0 %all-to-all-start = ((bf16[32,48,1024]{2,1,0:T(8,128)(2,1)}), bf16[32,48,1024]{2,1,0:T(8,128)(2,1)}, u32[]{:S(2)}, u32[]{:S(2)}) async-start(bf16[32,48,1024]{2,1,0:T(8,128)(2,1)} %get-tuple-element.31), calls=%async_computation | async-start | bytes 6291456 | tf_op jit(solution)/shard_map/all_to_all | solution.py:889
  214.4 3.8 %copy-start.14 = (bf16[1,128,1024]{2,1,0:T(8,128)(2,1)S(1)}, bf16[1,128,1024]{2,1,0:T(8,128)(2,1)}, u32[]{:S(2)}) copy-start(bf16[1,128,1024]{2,1,0:T(8,128)(2,1)} %param.17) | copy-start | bytes 786436
  215.3 3.1 %copy-start.1 = (bf16[2,4,4,2,16,1664]{5,4,3,2,1,0:T(8,128)(2,1)S(1)}, bf16[2,4,4,2,16,1664]{5,4,3,2,1,0:T(8,128)(2,1)}, u32[]{:S(2)}) copy-start(bf16[2,4,4,2,16,1664]{5,4,3,2,1,0:T(8,128)(2,1)} %get-tuple-element.28) | copy-start | bytes 10223620
  221.7 9.7 %copy-start.17 = (bf16[8,64,256]{2,1,0:T(8,128)(2,1)}, bf16[8,64,256]{2,1,0:T(8,128)(2,1)S(1)}, u32[]{:S(2)}) copy-start(bf16[8,64,256]{2,1,0:T(8,128)(2,1)S(1)} %fusion.23) | copy-start | bytes 786436
  242.8 42.2 %copy-start.9 = (f32[128,1024]{1,0:T(8,128)S(1)}, f32[128,1024]{1,0:T(8,128)}, u32[]{:S(2)}) copy-start(f32[128,1024]{1,0:T(8,128)} %get-tuple-element.74) | copy-start | bytes 1572868
  242.8 42.2 %copy-start.32 = (f32[1024,1]{0,1:T(1,128)S(1)}, f32[1024,1]{0,1:T(1,128)}, u32[]{:S(2)}) copy-start(f32[1024,1]{0,1:T(1,128)} %copy-done.31) | copy-start | bytes 12292
  242.8 42.4 %copy-start.40 = (f32[128]{0:T(128)S(1)}, f32[128]{0:T(128)}, u32[]{:S(2)}) copy-start(f32[128]{0:T(128)} %slice.123) | copy-start | bytes 1540
  288.7 6.4 %copy-start.12 = (f32[512,512]{1,0:T(8,128)S(1)}, f32[512,512]{1,0:T(8,128)}, u32[]{:S(2)}) copy-start(f32[512,512]{1,0:T(8,128)} %get-tuple-element.39) | copy-start | bytes 3145732
  292.0 4.1 %copy-start.11 = (f32[512,512]{1,0:T(8,128)S(1)}, f32[512,512]{1,0:T(8,128)}, u32[]{:S(2)}) copy-start(f32[512,512]{1,0:T(8,128)} %get-tuple-element.40) | copy-start | bytes 3145732
  (19 other events, 35.6 us)

commit v2 on v1

--- a/solution.py
+++ b/solution.py
@@ -37,11 +37,6 @@
 
 def rms_scale(values, gain):
     return values * lax.rsqrt(jnp.mean(values * values, axis=-1, keepdims=True) + epsilon) * gain
-
-
-def in_two(values):
-    high = lax.reduce_precision(values, 8, 7)
-    return high.astype(jnp.bfloat16), (values - high).astype(jnp.bfloat16)
 
 
 def rotate(values, cosine, sine_table):
@@ -529,6 +524,8 @@
     table_both,
     normed_both,
     grad_both,
+    grad_twice,
+    gated,
     picks,
     x_send,
     g_send,
@@ -635,17 +632,17 @@
     def send_g(chunk):
         @pl.loop(0, steps)
         def _(inner):
-            step = chunk * steps + inner
-            line = entry(step)
+            line = entry(chunk * steps + inner)
             weight = jnp.where(line[0:1] == place, line[1:2], 0.0)
             high = weight.astype(jnp.bfloat16)
             rest = (weight - high.astype(jnp.float32)).astype(jnp.bfloat16)
-            rows = pl.ds(pl.multiple_of(step * BLOCK, 16), BLOCK)
-            values = dot_plain(high, grad_both[step // PLANE]) + dot_plain(
-                rest, grad_both[step // PLANE]
-            )
-            g_send[rows, :] = values.astype(jnp.bfloat16)
-
+            rows = pl.ds(pl.multiple_of(inner * BLOCK, 16), BLOCK)
+            gated[rows, :rows_own] = high
+            gated[rows, rows_own:] = rest
+
+        g_send[g_rows.rows(chunk), :] = dot_plain(
+            gated[...], grad_twice[pl.ds(pl.multiple_of(chunk // 2 * 2 * rows_own, 16), 2 * rows_own)]
+        ).astype(jnp.bfloat16)
         g_rows.send(chunk)
 
     for chunk in (0, 1):
@@ -655,6 +652,8 @@
     for chunk in (2, 3):
         send_x(chunk)
     near[2].wait_recv()
+    for i in range(4):
+        grad_twice[pl.ds(i * rows_own, rows_own)] = grad_both[i // 2]
 
     @pl.loop(0, CHUNKS)
     def _(turn):
@@ -734,53 +733,56 @@
         columns = pl.ds(pl.multiple_of(at * half, half), half)
         return dot_left(hidden[:, pl.ds(start, half_down)], g_land[:, columns]), columns
 
-    def both_tiles(side, keep):
-        @pl.loop(0, half // tile)
-        def _(at):
-            for which in range(2):
-                keep(which, pl.ds(pl.multiple_of(at * tile, tile), tile), product(side, which, at))
-
-    def keep_other(which, rows, values):
-        pair_send[which, rows, :] = values.astype(jnp.bfloat16)
-
-    def keep_own(which, rows, values):
-        (d_gate, d_up)[which][rows, :] = values
-
-    both_tiles(1 - core, keep_other)
+    pairs, sums = [], []
+
+    def add_pair(k, mine_sum, sent, landed, seq_sent, seq_landed, own_part):
+        moved = remote(sent, landed, sum_sems.at[0, k], sum_sems.at[1, k], partner)
+        moved.start()
+        own_part()
+        moved.wait_recv()
+        seq_sent[...] = (mine_sum[...] + landed[...].astype(jnp.float32)).astype(jnp.bfloat16)
+        onward = remote(
+            seq_sent, seq_landed, sum_sems.at[0, 3 + k], sum_sems.at[1, 3 + k], other_seq
+        )
+        onward.start()
+        pairs.append(moved)
+        sums.append(onward)
 
     @pl.loop(0, width // half)
     def _(at):
         values, columns = product_down(1 - core, at)
         pair_send_down[:, columns] = values.astype(jnp.bfloat16)
 
-    pairs = [
-        remote(pair_send, pair_land, sum_sems.at[0, 0], sum_sems.at[1, 0], partner),
-        remote(pair_send_down, pair_land_down, sum_sems.at[0, 1], sum_sems.at[1, 1], partner),
-    ]
-    for moved in pairs:
-        moved.start()
-    both_tiles(core, keep_own)
-
-    @pl.loop(0, width // half)
-    def _(at):
-        values, columns = product_down(core, at)
-        d_down[:, columns] = values
-
-    pairs[0].wait_recv()
+    def own_down_part():
+        @pl.loop(0, width // half)
+        def _(at):
+            values, columns = product_down(core, at)
+            d_down[:, columns] = values
+
+    add_pair(
+        2, d_down, pair_send_down, pair_land_down, seq_send_down, seq_land_down, own_down_part
+    )
     for which, mine_sum in enumerate((d_gate, d_up)):
-        seq_send[which] = (mine_sum[...] + pair_land[which].astype(jnp.float32)).astype(
-            jnp.bfloat16
+
+        @pl.loop(0, half // tile)
+        def _(at):
+            rows = pl.ds(pl.multiple_of(at * tile, tile), tile)
+            pair_send[which, rows, :] = product(1 - core, which, at).astype(jnp.bfloat16)
+
+        def own_part(which=which, mine_sum=mine_sum):
+            @pl.loop(0, half // tile)
+            def _(at):
+                mine_sum[pl.ds(pl.multiple_of(at * tile, tile), tile), :] = product(core, which, at)
+
+        add_pair(
+            which,
+            mine_sum,
+            pair_send.at[which],
+            pair_land.at[which],
+            seq_send.at[which],
+            seq_land.at[which],
+            own_part,
         )
-    pairs[1].wait_recv()
-    seq_send_down[...] = (d_down[...] + pair_land_down[...].astype(jnp.float32)).astype(
-        jnp.bfloat16
-    )
-    sums = [
-        remote(seq_send, seq_land, sum_sems.at[0, 2], sum_sems.at[1, 2], other_seq),
-        remote(seq_send_down, seq_land_down, sum_sems.at[0, 3], sum_sems.at[1, 3], other_seq),
-    ]
-    for moved in sums:
-        moved.start()
 
     back_ref[...] = jnp.zeros_like(back_ref)
 
@@ -805,10 +807,10 @@
     over.wait_recv()
     back_ref[...] += back_sum_land[...].astype(jnp.float32)
 
-    sums[0].wait_recv()
+    for moved in sums:
+        moved.wait_recv()
     for which, mine_sum in enumerate((d_gate, d_up)):
         mine_sum[...] = seq_send[which].astype(jnp.float32) + seq_land[which].astype(jnp.float32)
-    sums[1].wait_recv()
     d_down[...] = seq_send_down[...].astype(jnp.float32) + seq_land_down[...].astype(jnp.float32)
     outs = out_rows.at[pl.ds(0, 2 * PLANE * CROSS)]
     remote(outs, outs, out_sems.at[0], out_sems.at[1], partner).wait()
@@ -841,6 +843,8 @@
             pltpu.VMEM((2, PLANE, *table.shape[1:]), high),
             pltpu.VMEM((2, rows, width), low),
             pltpu.VMEM((2, rows, width), low),
+            pltpu.VMEM((4 * rows, width), low),
+            pltpu.VMEM((slots // CHUNKS, 2 * rows), low),
             pltpu.VMEM((slots, rows), low),
             pltpu.VMEM((slots, width + SMALL), low),
             pltpu.VMEM((slots, width), low),
@@ -872,7 +876,7 @@
             dma((3, 2)),
             dma((2,)),
             dma((3, 3)),
-            dma((2, 4)),
+            dma((2, 6)),
             dma((2, 4)),
         ],
         compiler_params=pltpu.CompilerParams(
@@ -998,11 +1002,7 @@
     returned = from_experts(part_out).reshape(experts * places, width)
 
     gates_wide = jnp.where(onehot_wide, gates.T[:, None, :], 0.0)
-    gates_high, gates_rest = in_two(gates_wide)
-    flat = (experts * places, rows)
-    mixed = dot_left(gates_high.reshape(flat), returned) + dot_left(
-        gates_rest.reshape(flat), returned
-    )
+    mixed = dot_left(gates_wide.astype(jnp.bfloat16).reshape(experts * places, rows), returned)
     layer_out = (middle + mixed).astype(jnp.bfloat16)
     weighted = dots[:, :experts] + dots[:, experts : 2 * experts]
     grad_picked = weighted - gates * jnp.sum(weighted, axis=-1, keepdims=True)

time: 299 us -> 293 us (0.980)
  Pallas kernels: 221 us -> 216 us
    pallas_call x1, Pallas kernels: 139 us -> 135 us  [run_experts(): pl.pallas_call(expert_kernel, out_shape=[jax.ShapeDtypeStruct((chips, BLO...]
    dot_general x7 -> x6, matrix products: 11.3 us -> 8.83 us  [dot_left(): lax.dot_general(left, right, (((0,), (0,)), ((), ())), preferred_element_...]
    unnamed x94 -> x92, local copies, waits for them, and re-layouts: 8.44 us -> 8.44 us
where the time goes in v2:
time: 293 us; the launch traced here: 292 us
  Pallas kernels  216 us (74%)
  matrix products  32.5 us (11%)
  local copies, waits for them, and re-layouts  19.6 us (7%)
  other arithmetic  16.1 us (5%)
  starting transfers between devices  6.42 us (2%)
    pallas_call x1, Pallas kernels, run_experts(): pl.pallas_call(expert_kernel, out_shape=[jax.ShapeDtypeStruct((chips, BLO...  135 us
    pallas_call x1, Pallas kernels, scatter_sums(): pl.pallas_call(functools.partial(scatter_kernel, groups), out_shape=[jax....  41.2 us
    pallas_call x1, Pallas kernels, gather_shards(): pl.pallas_call(gather_kernel, out_shape=outs, in_specs=[ANY] * 4, out_spe...  39.9 us
    dot_general x6, matrix products, dot_left(): lax.dot_general(left, right, (((0,), (0,)), ((), ())), preferred_element_...  8.83 us
    unnamed x92, local copies, waits for them, and re-layouts  8.44 us
    dot_general x5, matrix products, dot_right(): lax.dot_general(left, right, (((1,), (1,)), ((), ())), preferred_element_...  8.12 us
    dot_general x6, matrix products, dot_plain(): return jnp.dot(left, right, preferred_element_type=jnp.float32)  7.15 us
    all_to_all x1, starting transfers between devices, from_experts(): lax.all_to_all(blocks, 'fsdp', split_axis=0, concat_axis=0, tiled=True, a...  6.42 us
  transfers between devices with their start and end apart: 1, of which 0 were waited for; matrix products, arithmetic and copies ran while one was open for 10% of the time, Pallas kernels for 14%

profile of v2, /device:TPU:1, one launch (start us, length us, event | category | flops | bytes accessed | tf_op | source)
XLA Modules:
  0.0 291.8 jit_solution(17432682595665410703)
XLA Ops:
  3.8 1.4 pad_maximum_fusion.1.shard_a
  5.2 1.5 concatenate.49.shard_b
  6.6 39.9 %gather_weights.1 = (bf16[2,4,4,2,16,1536]{5,4,3,2,1,0:T(8,128)(2,1)}, bf16[2,4,4,2,16,1664]{5,4,3,2,1,0:T(8,128)(2,1)}, bf16[128,1024]{1,0:T(8,128)(2,1)}, s32[1,128]{1,0:T(1,128)}) custom-call(bf16[16,1536]{1,0:T(8,128)(2,1)} %pad_maximum_fusion.1.shard_a, bf16[16,1664]{1,0:T(8,128)(2,1)} %concatenate.49.shard_b, bf16[128,1024]{1,0:T(8,128)(2,1)} %bitcast.156, ...), custom_call_target="tpu_custom_call" | custom-call | tf_op jit(solution)/shard_map/gather_weights/pallas_call | solution.py:216
  49.0 2.0 slice_convert_fusion.1
  51.5 2.5 convolution_convert_fusion.6
  54.0 1.7 fusion.11
  55.7 1.3 fusion.35
  58.7 1.8 copy.72
  62.9 2.1 fusion.77
  65.0 2.1 convolution_convert_fusion.5
  69.7 134.6 %experts.1 = (bf16[32,48,1024]{2,1,0:T(8,128)(2,1)}, f32[128,1152]{1,0:T(8,128)}, f32[512,512]{1,0:T(8,128)}, f32[512,512]{1,0:T(8,128)}, f32[256,1024]{1,0:T(8,128)}) custom-call(f32[32,2,128]{2,1,0:T(2,128)} %pad_maximum_fusion.2.table, bf16[128,1024]{1,0:T(8,128)(2,1)} %copy-done.3, bf16[128,1024]{1,0:T(8,128)(2,1)} %bitcast.169, ...), custom_call_target="tpu_custom_call" | custom-call | tf_op jit(solution)/shard_map/experts/pallas_call | solution.py:831
  204.4 6.4 %all-to-all-start = ((bf16[32,48,1024]{2,1,0:T(8,128)(2,1)}), bf16[32,48,1024]{2,1,0:T(8,128)(2,1)}, u32[]{:S(2)}, u32[]{:S(2)}) async-start(bf16[32,48,1024]{2,1,0:T(8,128)(2,1)} %get-tuple-element.31), calls=%async_computation | async-start | bytes 6291456 | tf_op jit(solution)/shard_map/all_to_all | solution.py:893
  212.7 2.1 multiply_reduce_fusion.2
  216.0 2.2 fusion.22
  221.8 1.7 copy.85
  223.5 1.8 concatenate.63
  226.2 1.7 fusion.33
  227.9 1.9 convolution_add_fusion
  230.3 1.6 fusion.39
  233.2 1.4 maximum_maximum_fusion.refs_4_
  234.5 1.4 convolution_convert_fusion.2
  236.5 2.1 convolution_convert_fusion
  239.3 41.2 %scatter_gradients.1 = (f32[16,1024]{1,0:T(8,128)S(1)}, f32[16,512]{1,0:T(8,128)S(1)}, f32[16,1024]{1,0:T(8,128)S(1)}, f32[16,512]{1,0:T(8,128)S(1)}, f32[16,128...) custom-call(bf16[128,1024]{1,0:T(8,128)(2,1)S(1)} %slice.230.before, bf16[2,4,4,2,16,1024]{5,4,3,2,1,0:T(8,128)(2,1)S(1)} %bitcast.144, ...), custom_call_target="tpu_custom_call" | custom-call | tf_op jit(solution)/shard_map/scatter_gradients/pallas_call | solution.py:398
  282.4 3.3 %fusion.29 = bf16[1,128,1024]{2,1,0:T(8,128)(2,1)} fusion(f32[128,1024]{1,0:T(8,128)S(1)} %get-tuple-element.68, bf16[32,48,1024]{2,1,0:T(8,128)(2,1)} %all-to-all-done, f32[32,128]{1,0:T(8,128)S(1)} %copy-done.29, s32[32,128]{1,0:T(8,128)S(1)} %copy-done.33), kind=kOutput, calls=%fused_computation.39 | convolution fusion | flops 403308544 | bytes 3964928 | tf_op jit(solution)/shard_map/dot_general | solution.py:27
  (149 shorter events, 30.5 us)
Async XLA Ops:
  46.5 4.7 %copy-start.2 = (bf16[1,128,1024]{2,1,0:T(8,128)(2,1)S(1)}, bf16[1,128,1024]{2,1,0:T(8,128)(2,1)}, u32[]{:S(2)}) copy-start(bf16[1,128,1024]{2,1,0:T(8,128)(2,1)} %param.14) | copy-start | bytes 786436
  46.6 4.7 %copy-start.5 = (bf16[128,1024]{1,0:T(8,128)(2,1)S(1)}, bf16[128,1024]{1,0:T(8,128)(2,1)}, u32[]{:S(2)}) copy-start(bf16[128,1024]{1,0:T(8,128)(2,1)} %get-tuple-element.27) | copy-start | bytes 786436
  51.2 2.8 copy-start.30
  51.2 2.7 copy-start.25
  54.0 3.1 %copy-start.38 = (s32[1,128]{1,0:T(1,128)S(1)}, s32[1,128]{1,0:T(1,128)}, u32[]{:S(2)}) copy-start(s32[1,128]{1,0:T(1,128)} %pos_own.1) | copy-start | bytes 1540
  54.0 3.1 %copy-start.40 = (s32[1,128]{1,0:T(1,128)S(1)}, s32[1,128]{1,0:T(1,128)}, u32[]{:S(2)}) copy-start(s32[1,128]{1,0:T(1,128)} %get-tuple-element.30) | copy-start | bytes 1540
  54.0 4.6 %copy-start.6 = (f32[1024,1]{1,0:T(8,128)S(1)}, f32[1024,1]{1,0:T(8,128)}, u32[]{:S(2)}) copy-start(f32[1024,1]{1,0:T(8,128)} %get-tuple-element.48) | copy-start | bytes 12292
  57.9 7.1 %copy-start.24 = (f32[256,32]{0,1:T(8,128)}, f32[256,32]{0,1:T(8,128)S(1)}, u32[]{:S(2)}) copy-start(f32[256,32]{0,1:T(8,128)S(1)} %get-tuple-element.64) | copy-start | bytes 98308
  61.6 3.4 %copy-start.22 = (bf16[256,8,32]{0,2,1:T(8,128)(2,1)}, bf16[256,8,32]{0,2,1:T(8,128)(2,1)S(1)}, u32[]{:S(2)}) copy-start(bf16[256,8,32]{0,2,1:T(8,128)(2,1)S(1)} %get-tuple-element.53) | copy-start | bytes 393220
  62.9 4.3 %copy-start.18 = (f32[128,16,32]{0,2,1:T(8,128)}, f32[128,16,32]{0,2,1:T(8,128)S(1)}, u32[]{:S(2)}) copy-start(f32[128,16,32]{0,2,1:T(8,128)S(1)} %get-tuple-element.56) | copy-start | bytes 786436
  62.9 4.3 %copy-start.20 = (f32[128,16,32]{0,2,1:T(8,128)}, f32[128,16,32]{0,2,1:T(8,128)S(1)}, u32[]{:S(2)}) copy-start(f32[128,16,32]{0,2,1:T(8,128)S(1)} %get-tuple-element.57) | copy-start | bytes 786436
  69.1 135.4 %copy-start.28 = (f32[32,128]{1,0:T(8,128)}, f32[32,128]{1,0:T(8,128)S(1)}, u32[]{:S(2)}) copy-start(f32[32,128]{1,0:T(8,128)S(1)} %fusion.65) | copy-start | bytes 49156
  204.4 6.5 %copy-start.37 = (f32[256]{0:T(256)S(1)}, f32[256]{0:T(256)}, u32[]{:S(2)}) copy-start(f32[256]{0:T(256)} %copy-done.36) | copy-start | bytes 3076
  204.4 7.1 %copy-start.13 = (f32[128,1152]{1,0:T(8,128)S(1)}, f32[128,1152]{1,0:T(8,128)}, u32[]{:S(2)}) copy-start(f32[128,1152]{1,0:T(8,128)} %get-tuple-element.32) | copy-start | bytes 1769476
  204.4 7.4 %copy-start.4 = (bf16[128,1024]{1,0:T(8,128)(2,1)S(1)}, bf16[128,1024]{1,0:T(8,128)(2,1)}, u32[]{:S(2)}) copy-start(bf16[128,1024]{1,0:T(8,128)(2,1)} %copy-done.3) | copy-start | bytes 786436
  204.4 78.0 %all-to-all-start = ((bf16[32,48,1024]{2,1,0:T(8,128)(2,1)}), bf16[32,48,1024]{2,1,0:T(8,128)(2,1)}, u32[]{:S(2)}, u32[]{:S(2)}) async-start(bf16[32,48,1024]{2,1,0:T(8,128)(2,1)} %get-tuple-element.31), calls=%async_computation | async-start | bytes 6291456 | tf_op jit(solution)/shard_map/all_to_all | solution.py:893
  210.9 3.9 %copy-start.14 = (bf16[1,128,1024]{2,1,0:T(8,128)(2,1)S(1)}, bf16[1,128,1024]{2,1,0:T(8,128)(2,1)}, u32[]{:S(2)}) copy-start(bf16[1,128,1024]{2,1,0:T(8,128)(2,1)} %param.17) | copy-start | bytes 786436
  211.8 3.1 %copy-start.1 = (bf16[2,4,4,2,16,1664]{5,4,3,2,1,0:T(8,128)(2,1)S(1)}, bf16[2,4,4,2,16,1664]{5,4,3,2,1,0:T(8,128)(2,1)}, u32[]{:S(2)}) copy-start(bf16[2,4,4,2,16,1664]{5,4,3,2,1,0:T(8,128)(2,1)} %get-tuple-element.28) | copy-start | bytes 10223620
  218.2 9.7 %copy-start.17 = (bf16[8,64,256]{2,1,0:T(8,128)(2,1)}, bf16[8,64,256]{2,1,0:T(8,128)(2,1)S(1)}, u32[]{:S(2)}) copy-start(bf16[8,64,256]{2,1,0:T(8,128)(2,1)S(1)} %fusion.22) | copy-start | bytes 786436
  239.3 42.0 %copy-start.9 = (f32[128,1024]{1,0:T(8,128)S(1)}, f32[128,1024]{1,0:T(8,128)}, u32[]{:S(2)}) copy-start(f32[128,1024]{1,0:T(8,128)} %get-tuple-element.74) | copy-start | bytes 1572868
  239.3 42.0 %copy-start.31 = (f32[1024,1]{0,1:T(1,128)S(1)}, f32[1024,1]{0,1:T(1,128)}, u32[]{:S(2)}) copy-start(f32[1024,1]{0,1:T(1,128)} %copy-done.30) | copy-start | bytes 12292
  239.3 42.1 %copy-start.39 = (f32[128]{0:T(128)S(1)}, f32[128]{0:T(128)}, u32[]{:S(2)}) copy-start(f32[128]{0:T(128)} %slice.123) | copy-start | bytes 1540
  282.4 6.4 %copy-start.12 = (f32[512,512]{1,0:T(8,128)S(1)}, f32[512,512]{1,0:T(8,128)}, u32[]{:S(2)}) copy-start(f32[512,512]{1,0:T(8,128)} %get-tuple-element.39) | copy-start | bytes 3145732
  285.7 4.1 %copy-start.11 = (f32[512,512]{1,0:T(8,128)S(1)}, f32[512,512]{1,0:T(8,128)}, u32[]{:S(2)}) copy-start(f32[512,512]{1,0:T(8,128)} %get-tuple-element.40) | copy-start | bytes 3145732
  (18 other events, 34.1 us)

commit v3 on v2

--- a/solution.py
+++ b/solution.py
@@ -84,8 +84,28 @@
     ]
 
 
-def gather_kernel(shard_a, shard_b, x_own, pos_own, full_a, full_b, x_other, pos_other, *sems):
+def gather_kernel(
+    w_query,
+    w_key,
+    w_value,
+    w_out,
+    small,
+    x_own,
+    pos_own,
+    full_a,
+    full_b,
+    x_other,
+    pos_other,
+    shard_a,
+    shard_b,
+    *sems,
+):
     send, recv, core_send, core_recv, seq_send, seq_recv, local = sems
+    for shard, pieces in ((shard_a, (w_query, w_key)), (shard_b, (w_value, w_out, small))):
+        at = 0
+        for piece in pieces:
+            shard[:, at : at + piece.shape[1]] = piece[...]
+            at += piece.shape[1]
     seq, y, x, z, core = coordinates()
     enter(neighbours())
     other_seq = device(1 - seq, y, x, z, core)
@@ -207,18 +227,23 @@
         moved.wait()
 
 
-def gather_shards(shard_a, shard_b, x_own, pos_own):
+def gather_shards(w_query, w_key, w_value, w_out, small, x_own, pos_own):
     count = lax.axis_size("fsdp")
     chips = (count // (LONG * LONG * CORES), LONG, LONG, CORES)
-    shards = (shard_a, shard_b)
+    height = w_query.shape[0]
+    shards = [
+        jax.ShapeDtypeStruct((height, sum(piece.shape[1] for piece in pieces)), w_query.dtype)
+        for pieces in ((w_query, w_key), (w_value, w_out, small))
+    ]
     outs = [jax.ShapeDtypeStruct((*chips, *shard.shape), shard.dtype) for shard in shards]
     outs += [jax.ShapeDtypeStruct(array.shape, array.dtype) for array in (x_own, pos_own)]
     full_a, full_b, x_other, pos_other = pl.pallas_call(
         gather_kernel,
         out_shape=outs,
-        in_specs=[ANY] * 4,
+        in_specs=[VMEM] * 5 + [ANY] * 2,
         out_specs=[ANY] * 4,
-        scratch_shapes=[
+        scratch_shapes=[pltpu.VMEM(shard.shape, shard.dtype) for shard in shards]
+        + [
             pltpu.SemaphoreType.DMA((2, 9)),
             pltpu.SemaphoreType.DMA((2, 9)),
             pltpu.SemaphoreType.DMA((2, 4)),
@@ -229,11 +254,10 @@
         ],
         compiler_params=pltpu.CompilerParams(collective_id=0, has_side_effects=True),
         name="gather_weights",
-    )(shard_a, shard_b, x_own, pos_own)
-    height = count * shard_a.shape[0]
+    )(w_query, w_key, w_value, w_out, small, x_own, pos_own)
     return (
-        full_a.reshape(height, shard_a.shape[1]),
-        full_b.reshape(height, shard_b.shape[1]),
+        full_a.reshape(count * height, full_a.shape[-1]),
+        full_b.reshape(count * height, full_b.shape[-1]),
         x_other,
         pos_other,
     )
@@ -895,6 +919,16 @@
     )
 
 
+def pack_small(router, first, second, shards):
+    rows, experts = router.shape
+    height = rows // shards
+    gains = jnp.concatenate(
+        [first.reshape(shards, 1, height), second.reshape(shards, 1, height)], axis=2
+    )
+    gains = jnp.pad(gains, ((0, 0), (0, height - 1), (0, SMALL - experts - 2 * height)))
+    return jnp.concatenate([router, gains.reshape(rows, SMALL - experts)], axis=1)
+
+
 def on_device(
     tokens,
     positions,
@@ -935,18 +969,13 @@
     grad_low = cotangent[0]
     grad_output = grad_low.astype(jnp.float32)
 
-    small = jnp.concatenate(
-        [
-            w_router,
-            first_gain[:, None],
-            second_gain[:, None],
-            jnp.zeros((w_router.shape[0], SMALL - experts - 2), jnp.bfloat16),
-        ],
-        axis=1,
-    )
+    small = pack_small(w_router, first_gain, second_gain, 1)
     full_a, full_b, x_before, pos_before = gather_shards(
-        jnp.concatenate([w_query, w_key], axis=1),
-        jnp.concatenate([w_value, w_out, small], axis=1),
+        w_query,
+        w_key,
+        w_value,
+        w_out,
+        small,
         x_own,
         positions,
     )
@@ -955,8 +984,10 @@
     out_full = full_b[:, kv_width : kv_width + width]
     small_full = full_b[:, kv_width + width :]
     router_full = small_full[:, :experts]
-    gain_first = small_full[:, experts].astype(jnp.float32)
-    gain_second = small_full[:, experts + 1].astype(jnp.float32)
+    height = w_router.shape[0]
+    gains = small_full.reshape(slots, height, SMALL)[:, 0, experts : experts + 2 * height]
+    gain_first = gains[:, :height].reshape(-1).astype(jnp.float32)
+    gain_second = gains[:, height:].reshape(-1).astype(jnp.float32)
 
     x_both = jnp.concatenate([x_before, x_own], axis=0).astype(jnp.float32)
     pos_both = jnp.concatenate([pos_before[0], positions[0]], axis=0)
@@ -1061,15 +1092,8 @@
     grad_gain_first = jnp.sum(grad_own * normed_x[rows:], axis=0) + jnp.sum(
         grad_both[:rows] * normed_x[:rows], axis=0
     )
-    small_grad = jnp.concatenate(
-        [
-            grad_router,
-            grad_gain_first[:, None],
-            grad_gain_second[:, None],
-            jnp.zeros((width, SMALL - experts - 2), jnp.float32),
-        ],
-        axis=1,
-    ).astype(jnp.bfloat16)
+    small_grad = pack_small(grad_router, grad_gain_first, grad_gain_second, slots)
+    small_grad = small_grad.astype(jnp.bfloat16)
     sum_out, sum_key, sum_query, sum_value, sum_small, grad_after = scatter_sums(
         [grad_out_full, grad_key_full, grad_query_full, grad_value_full, small_grad],
         (0, 0, 1, 1, 1),
@@ -1084,12 +1108,12 @@
     return (
         layer_out[None],
         grad_tokens[None],
-        sum_small[:, experts],
+        sum_small[0, experts : experts + height],
         sum_query,
         sum_key,
         sum_value,
         sum_out,
-        sum_small[:, experts + 1],
+        sum_small[0, experts + height : experts + 2 * height],
         sum_small[:, :experts],
         grad_gate[None],
         grad_up[None],

time: 293 us -> 288 us (0.983)
  local copies, waits for them, and re-layouts: 19.6 us -> 15.6 us
  Pallas kernels: 216 us -> 219 us
    concatenate x3 -> x0, local copies, waits for them, and re-layouts: 3.37 us -> none  [the longest x2 1.91 us: on_device(): jnp.concatenate([grad_router, grad_gain_first[:, None], grad_gain_second[...]
    unnamed x92 -> x89, local copies, waits for them, and re-layouts: 8.44 us -> 8.1 us
  transfers between devices with their start and end apart: 1 -> 1, of which waited for: 0 -> 0; matrix products, arithmetic and copies ran while one was open for 10% -> 9% of each run, Pallas kernels for 14% -> 15%
where the time goes in v3:
time: 288 us; the launch traced here: 287 us
  Pallas kernels  219 us (76%)
  matrix products  31.8 us (11%)
  local copies, waits for them, and re-layouts  15.6 us (5%)
  other arithmetic  13.5 us (5%)
  starting transfers between devices  5.85 us (2%)
    pallas_call x1, Pallas kernels, run_experts(): pl.pallas_call(expert_kernel, out_shape=[jax.ShapeDtypeStruct((chips, BLO...  134 us
    pallas_call x1, Pallas kernels, scatter_sums(): pl.pallas_call(functools.partial(scatter_kernel, groups), out_shape=[jax....  43.5 us
    pallas_call x1, Pallas kernels, gather_shards(): pl.pallas_call(gather_kernel, out_shape=outs, in_specs=[VMEM] * 5 + [ANY]...  41.1 us
    dot_general x6, matrix products, dot_left(): lax.dot_general(left, right, (((0,), (0,)), ((), ())), preferred_element_...  8.85 us
    dot_general x5, matrix products, dot_right(): lax.dot_general(left, right, (((1,), (1,)), ((), ())), preferred_element_...  8.11 us
    unnamed x89, local copies, waits for them, and re-layouts  8.1 us
    dot_general x6, matrix products, dot_plain(): return jnp.dot(left, right, preferred_element_type=jnp.float32)  6.35 us
    all_to_all x1, starting transfers between devices, from_experts(): lax.all_to_all(blocks, 'fsdp', split_axis=0, concat_axis=0, tiled=True, a...  5.85 us
  transfers between devices with their start and end apart: 1, of which 0 were waited for; matrix products, arithmetic and copies ran while one was open for 9% of the time, Pallas kernels for 15%

profile of v3, /device:TPU:1, one launch (start us, length us, event | category | flops | bytes accessed | tf_op | source)
XLA Modules:
  0.0 286.9 jit_solution(12203208058885063394)
XLA Ops:
  3.1 1.4 pad_maximum_fusion.4.small
  4.4 41.1 %gather_weights.1 = (bf16[2,4,4,2,16,1536]{5,4,3,2,1,0:T(8,128)(2,1)}, bf16[2,4,4,2,16,1664]{5,4,3,2,1,0:T(8,128)(2,1)}, bf16[128,1024]{1,0:T(8,128)(2,1)}, s32[1,128]{1,0:T(1,128)}) custom-call(bf16[16,1024]{1,0:T(8,128)(2,1)} %w_query.1, bf16[16,512]{1,0:T(8,128)(2,1)} %w_key.1, bf16[16,512]{1,0:T(8,128)(2,1)} %w_value.1, bf16[16,1024]{1,0:T(8,128)(2,1)} %w_out.1, ...), custom_call_target="tpu_custom_call" | custom-call | tf_op jit(solution)/shard_map/gather_weights/pallas_call | solution.py:240
  45.6 1.3 multiply_reduce_fusion
  46.8 1.1 maximum_convert_fusion
  49.6 2.5 convolution_convert_fusion.6
  52.1 1.7 fusion.11
  56.0 1.8 copy.83
  58.1 1.1 multiply_subtract_fusion.1
  59.2 2.1 fusion.84
  61.3 2.1 convolution_convert_fusion.5
  66.0 134.2 %experts.1 = (bf16[32,48,1024]{2,1,0:T(8,128)(2,1)}, f32[128,1152]{1,0:T(8,128)}, f32[512,512]{1,0:T(8,128)}, f32[512,512]{1,0:T(8,128)}, f32[256,1024]{1,0:T(8,128)}) custom-call(f32[32,2,128]{2,1,0:T(2,128)} %pad_maximum_fusion.2.table, bf16[128,1024]{1,0:T(8,128)(2,1)} %copy-done.3, bf16[128,1024]{1,0:T(8,128)(2,1)} %bitcast.177, ...), custom_call_target="tpu_custom_call" | custom-call | tf_op jit(solution)/shard_map/experts/pallas_call | solution.py:855
  200.3 5.8 %all-to-all-start = ((bf16[32,48,1024]{2,1,0:T(8,128)(2,1)}), bf16[32,48,1024]{2,1,0:T(8,128)(2,1)}, u32[]{:S(2)}, u32[]{:S(2)}) async-start(bf16[32,48,1024]{2,1,0:T(8,128)(2,1)} %get-tuple-element.31), calls=%async_computation | async-start | bytes 6291456 | tf_op jit(solution)/shard_map/all_to_all | solution.py:917
  207.9 2.1 multiply_reduce_fusion.2
  211.3 2.2 fusion.22
  215.9 1.1 fusion.26
  217.8 1.7 copy.96
  220.4 1.7 fusion.33
  222.1 1.9 convolution_add_fusion
  224.5 1.6 fusion.39
  226.4 1.1 pad_maximum_fusion.1.refs_4_
  227.5 1.4 convolution_convert_fusion.2
  229.5 2.1 convolution_convert_fusion
  232.3 43.5 %scatter_gradients.1 = (f32[16,1024]{1,0:T(8,128)S(1)}, f32[16,512]{1,0:T(8,128)S(1)}, f32[16,1024]{1,0:T(8,128)S(1)}, f32[16,512]{1,0:T(8,128)S(1)}, f32[16,128...) custom-call(bf16[128,1024]{1,0:T(8,128)(2,1)S(1)} %slice.237.before, bf16[2,4,4,2,16,1024]{5,4,3,2,1,0:T(8,128)(2,1)S(1)} %bitcast.151, ...), custom_call_target="tpu_custom_call" | custom-call | tf_op jit(solution)/shard_map/scatter_gradients/pallas_call | solution.py:422
  277.6 3.3 %fusion.29 = bf16[1,128,1024]{2,1,0:T(8,128)(2,1)} fusion(f32[128,1024]{1,0:T(8,128)S(1)} %get-tuple-element.68, bf16[32,48,1024]{2,1,0:T(8,128)(2,1)} %all-to-all-done, f32[32,128]{1,0:T(8,128)S(1)} %copy-done.28, s32[32,128]{1,0:T(8,128)S(1)} %copy-done.32), kind=kOutput, calls=%fused_computation.39 | convolution fusion | flops 403308544 | bytes 3964928 | tf_op jit(solution)/shard_map/dot_general | solution.py:27
  (150 shorter events, 25.6 us)
Async XLA Ops:
  0.6 48.7 %copy-start.2 = (bf16[1,128,1024]{2,1,0:T(8,128)(2,1)S(1)}, bf16[1,128,1024]{2,1,0:T(8,128)(2,1)}, u32[]{:S(2)}) copy-start(bf16[1,128,1024]{2,1,0:T(8,128)(2,1)} %param.14) | copy-start | bytes 786436
  45.5 3.8 %copy-start.5 = (bf16[128,1024]{1,0:T(8,128)(2,1)S(1)}, bf16[128,1024]{1,0:T(8,128)(2,1)}, u32[]{:S(2)}) copy-start(bf16[128,1024]{1,0:T(8,128)(2,1)} %get-tuple-element.27) | copy-start | bytes 786436
  48.0 4.1 %copy-start.35 = (f32[256]{0:T(256)}, f32[256]{0:T(256)S(1)}, u32[]{:S(2)}) copy-start(f32[256]{0:T(256)S(1)} %add_rsqrt_fusion) | copy-start | bytes 3076
  49.3 2.7 copy-start.29
  49.3 2.7 copy-start.24
  55.3 6.0 %copy-start.23 = (f32[256,32]{0,1:T(8,128)}, f32[256,32]{0,1:T(8,128)S(1)}, u32[]{:S(2)}) copy-start(f32[256,32]{0,1:T(8,128)S(1)} %get-tuple-element.64) | copy-start | bytes 98308
  57.9 3.4 %copy-start.21 = (bf16[256,8,32]{0,2,1:T(8,128)(2,1)}, bf16[256,8,32]{0,2,1:T(8,128)(2,1)S(1)}, u32[]{:S(2)}) copy-start(bf16[256,8,32]{0,2,1:T(8,128)(2,1)S(1)} %get-tuple-element.49) | copy-start | bytes 393220
  59.2 4.3 %copy-start.17 = (f32[128,16,32]{0,2,1:T(8,128)}, f32[128,16,32]{0,2,1:T(8,128)S(1)}, u32[]{:S(2)}) copy-start(f32[128,16,32]{0,2,1:T(8,128)S(1)} %get-tuple-element.52) | copy-start | bytes 786436
  59.2 4.3 %copy-start.19 = (f32[128,16,32]{0,2,1:T(8,128)}, f32[128,16,32]{0,2,1:T(8,128)S(1)}, u32[]{:S(2)}) copy-start(f32[128,16,32]{0,2,1:T(8,128)S(1)} %get-tuple-element.53) | copy-start | bytes 786436
  61.3 2.7 copy-start
  65.4 134.9 %copy-start.27 = (f32[32,128]{1,0:T(8,128)}, f32[32,128]{1,0:T(8,128)S(1)}, u32[]{:S(2)}) copy-start(f32[32,128]{1,0:T(8,128)S(1)} %fusion.65) | copy-start | bytes 49156
  200.2 5.9 %copy-start.36 = (f32[256]{0:T(256)S(1)}, f32[256]{0:T(256)}, u32[]{:S(2)}) copy-start(f32[256]{0:T(256)} %copy-done.35) | copy-start | bytes 3076
  200.2 6.5 %copy-start.12 = (f32[128,1152]{1,0:T(8,128)S(1)}, f32[128,1152]{1,0:T(8,128)}, u32[]{:S(2)}) copy-start(f32[128,1152]{1,0:T(8,128)} %get-tuple-element.32) | copy-start | bytes 1769476
  200.2 6.8 %copy-start.4 = (bf16[128,1024]{1,0:T(8,128)(2,1)S(1)}, bf16[128,1024]{1,0:T(8,128)(2,1)}, u32[]{:S(2)}) copy-start(bf16[128,1024]{1,0:T(8,128)(2,1)} %copy-done.3) | copy-start | bytes 786436
  200.3 77.3 %all-to-all-start = ((bf16[32,48,1024]{2,1,0:T(8,128)(2,1)}), bf16[32,48,1024]{2,1,0:T(8,128)(2,1)}, u32[]{:S(2)}, u32[]{:S(2)}) async-start(bf16[32,48,1024]{2,1,0:T(8,128)(2,1)} %get-tuple-element.31), calls=%async_computation | async-start | bytes 6291456 | tf_op jit(solution)/shard_map/all_to_all | solution.py:917
  206.1 3.9 %copy-start.13 = (bf16[1,128,1024]{2,1,0:T(8,128)(2,1)S(1)}, bf16[1,128,1024]{2,1,0:T(8,128)(2,1)}, u32[]{:S(2)}) copy-start(bf16[1,128,1024]{2,1,0:T(8,128)(2,1)} %param.17) | copy-start | bytes 786436
  207.1 3.1 %copy-start.1 = (bf16[2,4,4,2,16,1664]{5,4,3,2,1,0:T(8,128)(2,1)S(1)}, bf16[2,4,4,2,16,1664]{5,4,3,2,1,0:T(8,128)(2,1)}, u32[]{:S(2)}) copy-start(bf16[2,4,4,2,16,1664]{5,4,3,2,1,0:T(8,128)(2,1)} %get-tuple-element.28) | copy-start | bytes 10223620
  213.5 8.6 %copy-start.16 = (bf16[8,64,256]{2,1,0:T(8,128)(2,1)}, bf16[8,64,256]{2,1,0:T(8,128)(2,1)S(1)}, u32[]{:S(2)}) copy-start(bf16[8,64,256]{2,1,0:T(8,128)(2,1)S(1)} %fusion.22) | copy-start | bytes 786436
  228.9 2.6 copy-start.15
  232.2 43.5 %copy-start.8 = (f32[128,1024]{1,0:T(8,128)S(1)}, f32[128,1024]{1,0:T(8,128)}, u32[]{:S(2)}) copy-start(f32[128,1024]{1,0:T(8,128)} %get-tuple-element.74) | copy-start | bytes 1572868
  232.2 43.5 %copy-start.30 = (f32[1024]{0:T(1024)S(1)}, f32[1024]{0:T(1024)}, u32[]{:S(2)}) copy-start(f32[1024]{0:T(1024)} %copy-done.29) | copy-start | bytes 12292
  232.3 44.3 %copy-start.38 = (f32[128]{0:T(128)S(1)}, f32[128]{0:T(128)}, u32[]{:S(2)}) copy-start(f32[128]{0:T(128)} %slice.128) | copy-start | bytes 1540
  277.6 6.4 %copy-start.11 = (f32[512,512]{1,0:T(8,128)S(1)}, f32[512,512]{1,0:T(8,128)}, u32[]{:S(2)}) copy-start(f32[512,512]{1,0:T(8,128)} %get-tuple-element.39) | copy-start | bytes 3145732
  280.9 4.1 %copy-start.10 = (f32[512,512]{1,0:T(8,128)S(1)}, f32[512,512]{1,0:T(8,128)}, u32[]{:S(2)}) copy-start(f32[512,512]{1,0:T(8,128)} %get-tuple-element.40) | copy-start | bytes 3145732
  (17 other events, 30.8 us)
